TPU v7x, 32 devices: a whole 2x2x4 slice. The times are simulated.
32 devices in a mesh: species: 4 (over z), mode: 4 (over y, x), space: 2 (over core).
Axes of the slice: x: 2, y: 2, z: 4, core: 2. Of those that a mesh axis runs over, the one named last changes fastest.
Arguments:
- distribution: float32 [8, 1024, 2, 512], P('species', 'mode', 'space'), may hold values from -6 to 6
- kernel: bfloat16 [2, 120, 120, 120], P(None, 'mode'), may hold values from -0.046875 to 0.046875
- pair_kind: int32 [8, 8], replicated, may hold values from 0 to 1
- low_map: int32 [120], replicated, may hold values from 0 to 448, as said below
- thermal_speed: float32 [8], P('species'), may hold values from 0.5 to 1
- relax_rate: float32 [8], P('species'), may hold values from 2 to 8
Outputs:
- updated: float32 [8, 1024, 2, 512], P('species', 'mode', 'space')
Inputs may be any that keep to these rules, and one draw needn't show every extreme that they name: low_map lists each of the 120 modes whose degrees a, b, c sum to at most 7 exactly once, in some order; a mode's index is a * 8 * 8 + b * 8 + c.
All inputs are finite; a program needn't handle non-finite values.
Results may differ from a plain program's by a relative error of at most 0.0025.
Values may be sent and summed in bfloat16 or wider, within the bound.
A program may use at most 128 MiB of HBM per device.

v0:
```python
import functools

import jax
import jax.numpy as jnp
import numpy as np
from jax import lax
from jax.experimental import pallas as pl
from jax.experimental.pallas import tpu as pltpu
from jax.sharding import PartitionSpec as P

MESH = pl.DeviceIdType.MESH
F32 = jnp.float32
BF16 = jnp.bfloat16

NVY = 8
NVZ = 8
DEG = 7
NKIND = 2
NY = 256

nu_step = 0.0625
dt_step = 0.05
bound_x = 6.7
bound_y = 4.2
bound_z = 4.2

SPLIT = 4
OWN = 2
ROWS = 256
PER_VX = 4
LANES = 128
HEAD = 208
PACK = 256
PIECE = 64
PAD_J = 128
PAD_N = 32


def packed_table():
    low = [
        (a * NVY + b) * NVZ + c
        for a in range(DEG + 1)
        for b in range(NVY)
        for c in range(NVZ)
        if a + b + c <= DEG
    ]
    table = np.full((PACK, 8), -1, np.int32)
    for start, first in ((0, 0), (HEAD, ROWS)):
        held = [mode for mode in low if first <= mode < first + ROWS]
        row = start
        for slot in range(OWN):
            for mode in held:
                table[row, 0] = slot * ROWS + mode - first
                table[row, 1 + slot] = mode
                row += 1
        assert row <= (HEAD if start == 0 else PACK)
    return table


def dot(left, right):
    return jnp.dot(left, right, preferred_element_type=F32)


def kernel(
    space_count,
    f_in,
    k_in,
    tab_ref,
    lm_ref,
    kind_ref,
    th_ref,
    rx_ref,
    out_ref,
    f_ref,
    kraw,
    k2,
    low_send,
    full,
    low,
    pmat,
    gsum,
    gsend,
    grecv,
    pick,
    spread,
    halo_send,
    halo_recv,
    ab_send,
    ab_recv,
    copy_sem,
    s1,
    r1,
    s2,
    r2,
    s3,
    r3,
    hs,
    hr,
    xs,
    xr,
):
    q = lax.axis_index("species")
    m = lax.axis_index("mode")
    sx = lax.axis_index("space")

    copy_f = pltpu.make_async_copy(f_in, f_ref, copy_sem.at[0])
    copy_k = pltpu.make_async_copy(k_in, kraw, copy_sem.at[1])
    copy_f.start()
    copy_k.start()

    barrier = pltpu.get_barrier_semaphore()
    for step in range(1, SPLIT * SPLIT):
        other = lax.rem(q * SPLIT + m + step, SPLIT * SPLIT)
        pl.semaphore_signal(
            barrier,
            inc=1,
            device_id={"species": other // SPLIT, "mode": lax.rem(other, SPLIT)},
            device_id_type=MESH,
        )

    @pl.when(sx > 0)
    def _():
        pl.semaphore_signal(barrier, inc=1, device_id={"space": sx - 1}, device_id_type=MESH)

    @pl.when(sx < space_count - 1)
    def _():
        pl.semaphore_signal(barrier, inc=1, device_id={"space": sx + 1}, device_id_type=MESH)

    copy_f.wait()

    def extract(first, count):
        rows = lax.broadcasted_iota(jnp.int32, (count, OWN * ROWS), 1)
        chosen = jnp.where(tab_ref[first : first + count, 0:1] == rows, 1.0, 0.0).astype(BF16)
        field = f_ref[...].reshape(OWN * ROWS, SPLIT * LANES).astype(BF16)
        packed = dot(chosen, field).astype(BF16)
        for part in range(SPLIT):
            low_send[part, first : first + count, :] = packed[:, part * LANES : (part + 1) * LANES]

    @pl.when(m == 0)
    def _():
        extract(0, HEAD)

    @pl.when(m == 1)
    def _():
        extract(HEAD, PACK - HEAD)

    for slot in range(OWN):
        halo_send[0, slot] = f_ref[slot, 0:64, :].astype(BF16)
        halo_send[1, slot] = f_ref[slot, ROWS - 64 : ROWS, :].astype(BF16)

    inner = (sx > 0) & (sx < space_count - 1)
    peers = SPLIT * SPLIT - 1

    @pl.when(inner)
    def _():
        pl.semaphore_wait(barrier, peers + 2)

    @pl.when(jnp.logical_not(inner))
    def _():
        pl.semaphore_wait(barrier, peers + min(1, space_count - 1))

    def scatter(part, piece, first, count, source):
        return pltpu.make_async_remote_copy(
            src_ref=low_send.at[part, pl.ds(first, count)],
            dst_ref=full.at[q, pl.ds(first, count)],
            send_sem=s1.at[part, piece],
            recv_sem=r1.at[q, source],
            device_id={"species": part, "mode": piece},
            device_id_type=MESH,
        )

    head_last = HEAD - 3 * PIECE

    def head_copies(step):
        part = lax.rem(q + step, SPLIT)
        found = []
        for piece in (3, 1, 2, 0):
            if step == 0 and piece == 0:
                continue
            count = PIECE if piece < 3 else head_last
            found.append(scatter(part, piece, piece * PIECE, count, 0))
        return found

    def tail_copies(step):
        return scatter(lax.rem(q + step, SPLIT), 3, HEAD, PACK - HEAD, 1)

    @pl.when(m == 0)
    def _():
        for step in (1, 2, 3, 0):
            for item in head_copies(step):
                item.start()
        full[q, 0:PIECE, :] = low_send[q, 0:PIECE, :]

    @pl.when(m == 1)
    def _():
        for step in (1, 2, 3, 0):
            tail_copies(step).start()

    def halo(way):
        return pltpu.make_async_remote_copy(
            src_ref=halo_send.at[way],
            dst_ref=halo_recv.at[1 - way],
            send_sem=hs.at[way],
            recv_sem=hr.at[1 - way],
            device_id={"mode": m - 1 if way == 0 else m + 1},
            device_id_type=MESH,
        )

    @pl.when(m >= 2)
    def _():
        halo(0).start()

    @pl.when(m == 2)
    def _():
        halo(1).start()

    copy_k.wait()

    def lay(n, carry):
        k2[n] = jnp.zeros((PAD_J, NKIND * PAD_J), BF16)

        @pl.when(n < kraw.shape[1])
        def _():
            spot = jnp.minimum(n, kraw.shape[1] - 1)
            for kind in range(NKIND):
                k2[n, 0 : kraw.shape[2], kind * PAD_J : kind * PAD_J + kraw.shape[3]] = kraw[
                    kind, spot
                ]

        return carry

    lax.fori_loop(0, PAD_N, lay, 0)

    for slot in range(OWN):
        same = tab_ref[:, 1 + slot : 2 + slot] == lm_ref[0:1, :]
        pick[slot] = jnp.where(same, 1.0, 0.0).T.astype(BF16)
    mode_of = lax.broadcasted_iota(jnp.int32, (ROWS, PAD_J), 0) + m * ROWS
    spread[...] = jnp.where(mode_of == lm_ref[1:2, :], 1.0, 0.0).astype(BF16)

    def piece_wait(source, count, sender):
        pltpu.make_async_remote_copy(
            src_ref=low_send.at[0, pl.ds(0, count)],
            dst_ref=full.at[source, pl.ds(0, count)],
            send_sem=s1.at[0, 0],
            recv_sem=r1.at[source, sender],
            device_id={"mode": lax.rem(m + 1, SPLIT)},
            device_id_type=MESH,
        ).wait_recv()

    def forward(source, step):
        rows = pl.ds(pl.multiple_of(m * PIECE, PIECE), PIECE)
        return pltpu.make_async_remote_copy(
            src_ref=full.at[source, rows],
            dst_ref=full.at[source, rows],
            send_sem=s2.at[source, step],
            recv_sem=r2.at[source, m],
            device_id={"mode": lax.rem(m + step, SPLIT)},
            device_id_type=MESH,
        )

    for back in range(SPLIT):
        source = lax.rem(q + SPLIT - back, SPLIT)

        if back > 0:

            @pl.when(m == 0)
            def _():
                piece_wait(source, PIECE, 0)

        @pl.when((m == 1) | (m == 2))
        def _():
            piece_wait(source, PIECE, 0)

        @pl.when(m == 3)
        def _():
            piece_wait(source, head_last, 0)
            piece_wait(source, PACK - HEAD, 1)

        for step in range(1, SPLIT):
            forward(source, step).start()

    @pl.when(m < 2)
    def _():
        halo(1).start()

    @pl.when(m == 1)
    def _():
        halo(0).start()

    degree_c = lax.broadcasted_iota(jnp.int32, (NVZ, 1), 0)
    sqrt_c = jnp.sqrt(degree_c.astype(F32))
    sqrt_c_up = jnp.where(degree_c == NVZ - 1, 0.0, jnp.sqrt(degree_c.astype(F32) + 1.0))
    planes = SPLIT * LANES // NY

    def own_terms(i, carry):
        slot = i // PER_VX
        a = lax.rem(i, PER_VX)
        scale = nu_step * th_ref[slot]
        relax = dt_step * rx_ref[slot]
        blocks = [
            f_ref[slot, pl.ds(pl.multiple_of(a * 64 + b * NVZ, NVZ), NVZ), :] for b in range(NVY)
        ]
        for b in range(NVY):
            here = blocks[b]
            flux_y = jnp.zeros_like(here)
            if b < NVY - 1:
                flux_y = flux_y + float(np.sqrt(np.float32(b + 1))) * blocks[b + 1]
            if b > 0:
                flux_y = flux_y + float(np.sqrt(np.float32(b))) * blocks[b - 1]
            up_y = 0.5 * flux_y - 0.5 * bound_y * here
            down_y = -0.5 * flux_y - 0.5 * bound_y * here
            turned = []
            for plane in range(planes):
                cut = slice(plane * NY, (plane + 1) * NY)
                turned.append(
                    pltpu.roll(up_y[:, cut], NY - 1, 1) + pltpu.roll(down_y[:, cut], 1, 1)
                )
            y_term = jnp.concatenate(turned, axis=1) + bound_y * here
            flux_z = sqrt_c_up * pltpu.roll(here, NVZ - 1, 0) + sqrt_c * pltpu.roll(here, 1, 0)
            wide = planes * NY
            up_z = 0.5 * flux_z - 0.5 * bound_z * here
            down_z = -0.5 * flux_z - 0.5 * bound_z * here
            z_term = (
                pltpu.roll(up_z, wide - NY, 1) + pltpu.roll(down_z, NY, 1) + bound_z * here
            )
            total = degree_c + (b + a + m * PER_VX)
            lost = jnp.where(total > DEG, relax, 0.0)
            out_ref[slot, pl.ds(pl.multiple_of(a * 64 + b * NVZ, NVZ), NVZ), :] = (
                here - scale * (y_term + z_term + bound_x * here) - lost * here
            )
        return carry

    lax.fori_loop(0, OWN * PER_VX, own_terms, 0)

    def x_parts(a):
        degree = (m * PER_VX + a).astype(F32)
        root = jnp.sqrt(jnp.full((8, 128), degree, F32))[0:1, 0:1]
        root_up = jnp.sqrt(jnp.full((8, 128), degree + 1.0, F32))[0:1, 0:1]

        def part(i, carry):
            slot = i // 4
            r = lax.rem(i, 4) * 16
            here = f_ref[slot, pl.ds(pl.multiple_of(a * 64 + r, 16), 16), :]
            if a < PER_VX - 1:
                above = f_ref[slot, pl.ds(pl.multiple_of((a + 1) * 64 + r, 16), 16), :]
            else:
                above = halo_recv[1, slot, pl.ds(pl.multiple_of(r, 16), 16), :].astype(F32)
            if a > 0:
                below = f_ref[slot, pl.ds(pl.multiple_of((a - 1) * 64 + r, 16), 16), :]
            else:
                below = halo_recv[0, slot, pl.ds(pl.multiple_of(r, 16), 16), :].astype(F32)
            flux = root_up * above + root * below
            rows = pl.ds(pl.multiple_of(slot * 64 + r, 16), 16)
            ab_send[0, a, rows, :] = (0.5 * flux - 0.5 * bound_x * here).astype(ab_send.dtype)
            ab_send[1, a, rows, :] = (-0.5 * flux - 0.5 * bound_x * here).astype(ab_send.dtype)
            return carry

        lax.fori_loop(0, OWN * 4, part, 0)

    def layer(way, a):
        return pltpu.make_async_remote_copy(
            src_ref=ab_send.at[way, a],
            dst_ref=ab_recv.at[way, a],
            send_sem=xs.at[way, a],
            recv_sem=xr.at[way, a],
            device_id={"space": sx - 1 if way == 0 else sx + 1},
            device_id_type=MESH,
        )

    def send_layers(a):
        @pl.when(sx > 0)
        def _():
            layer(0, a).start()

        @pl.when(sx < space_count - 1)
        def _():
            layer(1, a).start()

    @pl.when(sx == space_count - 1)
    def _():
        ab_recv[0] = jnp.zeros(ab_recv.shape[1:], ab_recv.dtype)

    @pl.when(sx == 0)
    def _():
        ab_recv[1] = jnp.zeros(ab_recv.shape[1:], ab_recv.dtype)

    for a in (1, 2):
        x_parts(a)
        send_layers(a)

    def forward_wait(source, step):
        sender = lax.rem(m + step, SPLIT)
        pltpu.make_async_remote_copy(
            src_ref=full.at[source, pl.ds(0, PIECE)],
            dst_ref=full.at[source, pl.ds(0, PIECE)],
            send_sem=s2.at[source, step],
            recv_sem=r2.at[source, sender],
            device_id={"mode": sender},
            device_id_type=MESH,
        ).wait_recv()

    for back in range(SPLIT):
        source = lax.rem(q + SPLIT - back, SPLIT)
        for step in range(1, SPLIT):
            forward_wait(source, step)
        packed = full[source]
        for slot in range(OWN):
            low[source, :, slot * LANES : (slot + 1) * LANES] = dot(pick[slot], packed)

    def partners(pair, carry):
        for slot in range(OWN):
            sums = [jnp.zeros((PAD_J, LANES), F32) for _ in range(NKIND)]
            for r in range(SPLIT * OWN):
                values = low[r // OWN, :, (r % OWN) * LANES : (r % OWN + 1) * LANES]
                kind_here = kind_ref[pair * OWN + slot, r]
                for kind in range(NKIND):
                    sums[kind] = sums[kind] + jnp.where(kind_here == kind, 1.0, 0.0) * values
            for kind in range(NKIND):
                pmat[
                    pair,
                    kind * PAD_J : (kind + 1) * PAD_J,
                    slot * LANES : (slot + 1) * LANES,
                ] = sums[kind].astype(BF16)
        return carry

    lax.fori_loop(0, SPLIT, partners, 0)

    def give(pair, target):
        return pltpu.make_async_remote_copy(
            src_ref=gsend.at[pair],
            dst_ref=grecv.at[q, pl.ds(pl.multiple_of(m * PAD_N, PAD_N), PAD_N)],
            send_sem=s3.at[pair, target],
            recv_sem=r3.at[q, m],
            device_id={"species": pair, "mode": target},
            device_id_type=MESH,
        )

    group = 8

    def collide(pair):
        def some(i, carry):
            left = k2[pl.ds(pl.multiple_of(i * group, group), group)]
            product = dot(left.reshape(group * PAD_J, NKIND * PAD_J), pmat[pair])
            own = low[pair]
            gsum[pl.ds(pl.multiple_of(i * group, group), group), :] = jnp.sum(
                product.reshape(group, PAD_J, OWN * LANES) * own[None], axis=1
            )
            return carry

        lax.fori_loop(0, PAD_N // group, some, 0)
        gsend[pair] = gsum[...].astype(BF16)

    for step in (1, 2, 3, 0):
        pair = lax.rem(q + step, SPLIT)
        collide(pair)
        for target in range(2):
            if step > 0:
                give(pair, target).start()
            else:

                @pl.when(m != target)
                def _():
                    give(pair, target).start()

                @pl.when(m == target)
                def _():
                    grecv[q, target * PAD_N : (target + 1) * PAD_N, :] = gsend[pair]

    @pl.when(m > 0)
    def _():
        halo(1).wait_recv()

    @pl.when(m == 0)
    def _():
        halo_recv[0] = jnp.zeros(halo_recv.shape[1:], BF16)

    @pl.when(m < SPLIT - 1)
    def _():
        halo(0).wait_recv()

    @pl.when(m == SPLIT - 1)
    def _():
        halo_recv[1] = jnp.zeros(halo_recv.shape[1:], BF16)

    for a in (0, 3):
        x_parts(a)
        send_layers(a)

    for a in (1, 2, 0, 3):

        @pl.when(sx < space_count - 1)
        def _():
            layer(0, a).wait_recv()

        @pl.when(sx > 0)
        def _():
            layer(1, a).wait_recv()

        def add_x(i, carry):
            slot = i // 4
            r = lax.rem(i, 4) * 16
            rows = pl.ds(pl.multiple_of(slot * 64 + r, 16), 16)
            here = pl.ds(pl.multiple_of(a * 64 + r, 16), 16)
            term = ab_recv[0, a, rows, :].astype(F32) + ab_recv[1, a, rows, :].astype(F32)
            out_ref[slot, here, :] = out_ref[slot, here, :] - (nu_step * th_ref[slot]) * term
            return carry

        lax.fori_loop(0, OWN * 4, add_x, 0)

    @pl.when(m < 2)
    def _():
        for back in range(SPLIT):
            source = lax.rem(q + SPLIT - back, SPLIT)
            for sender in range(SPLIT):

                def take():
                    pltpu.make_async_remote_copy(
                        src_ref=gsend.at[0],
                        dst_ref=grecv.at[source, pl.ds(sender * PAD_N, PAD_N)],
                        send_sem=s3.at[0, 0],
                        recv_sem=r3.at[source, sender],
                        device_id={"mode": lax.rem(m + 1, SPLIT)},
                        device_id_type=MESH,
                    ).wait_recv()

                if back > 0 or sender > 1:
                    take()
                else:
                    pl.when(m != sender)(take)
            columns = pl.ds(pl.multiple_of(source * LANES, LANES), LANES)
            for slot in range(OWN):
                gained = dot(spread[...], grecv[source, :, slot * LANES : (slot + 1) * LANES])
                out_ref[slot, :, columns] = out_ref[slot, :, columns] + dt_step * gained

    @pl.when(m == 0)
    def _():
        for step in range(SPLIT):
            for item in head_copies(step):
                item.wait_send()

    @pl.when(m == 1)
    def _():
        for step in range(SPLIT):
            tail_copies(step).wait_send()

    for back in range(SPLIT):
        for step in range(1, SPLIT):
            forward(lax.rem(q + SPLIT - back, SPLIT), step).wait_send()

    @pl.when(m > 0)
    def _():
        halo(0).wait_send()

    @pl.when(m < SPLIT - 1)
    def _():
        halo(1).wait_send()

    for a in range(PER_VX):

        @pl.when(sx > 0)
        def _():
            layer(0, a).wait_send()

        @pl.when(sx < space_count - 1)
        def _():
            layer(1, a).wait_send()

    for step in range(SPLIT):
        pair = lax.rem(q + step, SPLIT)
        for target in range(2):
            if step > 0:
                give(pair, target).wait_send()
            else:

                @pl.when(m != target)
                def _():
                    give(pair, target).wait_send()


def per_device(space_count, distribution, kernels, pair_kind, low_map, thermal_speed, relax_rate):
    own, rows, layers, cells = distribution.shape
    assert (own, rows, layers, cells) == (OWN, ROWS, 1, SPLIT * LANES)
    kinds, out_rows, low_count, _ = kernels.shape
    field = distribution.reshape(own, rows, cells)
    ordered = jnp.pad(low_map, (0, PAD_J - low_count), constant_values=-2)
    by_block = jnp.pad(
        low_map.reshape(SPLIT, out_rows), ((0, 0), (0, PAD_N - out_rows)), constant_values=-2
    ).reshape(PAD_J)
    maps = jnp.stack([ordered, by_block])
    table = jnp.asarray(packed_table())
    vmem = pl.BlockSpec(memory_space=pltpu.VMEM)
    smem = pl.BlockSpec(memory_space=pltpu.SMEM)
    anywhere = pl.BlockSpec(memory_space=pl.ANY)
    dma = pltpu.SemaphoreType.DMA
    ab_type = F32
    result = pl.pallas_call(
        functools.partial(kernel, space_count),
        out_shape=jax.ShapeDtypeStruct((own, rows, cells), F32),
        in_specs=[anywhere, anywhere, vmem, vmem, smem, smem, smem],
        out_specs=vmem,
        scratch_shapes=[
            pltpu.VMEM((own, rows, cells), F32),
            pltpu.VMEM(kernels.shape, BF16),
            pltpu.VMEM((PAD_N, PAD_J, kinds * PAD_J), BF16),
            pltpu.VMEM((SPLIT, PACK, LANES), BF16),
            pltpu.VMEM((SPLIT, PACK, LANES), BF16),
            pltpu.VMEM((SPLIT, PAD_J, own * LANES), F32),
            pltpu.VMEM((SPLIT, kinds * PAD_J, own * LANES), BF16),
            pltpu.VMEM((PAD_N, own * LANES), F32),
            pltpu.VMEM((SPLIT, PAD_N, own * LANES), BF16),
            pltpu.VMEM((SPLIT, SPLIT * PAD_N, own * LANES), BF16),
            pltpu.VMEM((own, PAD_J, PACK), BF16),
            pltpu.VMEM((ROWS, PAD_J), BF16),
            pltpu.VMEM((2, own, 64, cells), BF16),
            pltpu.VMEM((2, own, 64, cells), BF16),
            pltpu.VMEM((2, PER_VX, own * 64, cells), ab_type),
            pltpu.VMEM((2, PER_VX, own * 64, cells), ab_type),
            dma((2,)),
            dma((SPLIT, SPLIT)),
            dma((SPLIT, 2)),
            dma((SPLIT, SPLIT)),
            dma((SPLIT, SPLIT)),
            dma((SPLIT, 2)),
            dma((SPLIT, SPLIT)),
            dma((2,)),
            dma((2,)),
            dma((2, PER_VX)),
            dma((2, PER_VX)),
        ],
        compiler_params=pltpu.CompilerParams(
            collective_id=0, has_side_effects=True, vmem_limit_bytes=48 * 1024 * 1024
        ),
    )(field, kernels, table, maps, pair_kind, thermal_speed, relax_rate)
    return result.reshape(own, rows, layers, cells)


def solution(mesh):
    in_specs = (
        P("species", "mode", "space", None),
        P(None, "mode", None, None),
        P(),
        P(),
        P("species"),
        P("species"),
    )
    out_specs = P("species", "mode", "space", None)
    return jax.shard_map(
        functools.partial(per_device, mesh.shape["space"]),
        mesh=mesh,
        in_specs=in_specs,
        out_specs=out_specs,
        check_vma=False,
    )
```

profile of v0, /device:TPU:0, one launch (start us, length us, event | category | flops | bytes accessed | tf_op | source)
XLA Modules:
  0.0 33.0 jit_solution(15317352893649897944)
XLA Ops:
  0.0 0.0 copy-start.1
  0.0 0.0 copy-start.4
  0.0 0.0 copy-start.3
  0.0 0.0 copy-start.2
  0.0 0.0 copy-start
  0.0 0.8 %pad_bitcast_fusion = s32[1,128]{1,0:T(1,128)S(1)} fusion(s32[120]{0:T(128)} %param.10), kind=kLoop, calls=%fused_computation.2 | loop fusion | bytes 992 | tf_op jit(solution)/shard_map/stack | solution.py:589
  0.8 0.7 %reshape.10 = s32[4,30]{1,0:T(4,128)S(1)} reshape(s32[120]{0:T(128)} %param.10) | data formatting | bytes 960 | tf_op jit(solution)/shard_map/reshape | solution.py:587
  1.6 0.1 stack_reshape.3
  1.7 1.3 %copy.11 = f32[2,256,1,512]{3,1,2,0:T(8,128)S(1)} copy(f32[2,256,1,512]{3,2,1,0:T(1,128)} %param.7) | data formatting | bytes 2097152
  3.0 0.0 copy-done.1
  3.0 0.0 copy-done.4
  3.0 0.0 copy-done.3
  3.0 0.0 copy-done.2
  3.0 0.0 copy-done
  3.0 28.0 %shard_map.73 = f32[2,256,512]{2,1,0:T(8,128)S(1)} custom-call(f32[2,256,512]{2,1,0:T(8,128)S(1)} %bitcast.7, bf16[2,30,120,120]{3,2,1,0:T(8,128)(2,1)S(1)} %copy-done, s32[256,8]{1,0:T(8,128)S(1)} %copy-done.1, s32[2,128]{1,0:T(2,128)S(1)} %pad_add_fusion.lm_ref, s32[8,8]{1,0:T(8,128)S(1)} %copy-done.2, f32[2]{0:T(128)S(1)} %copy-done.3, f32[2]{0:T(128)S(1)} %copy-done.4), custom_call_target="tpu_custom_call" | custom-call | tf_op jit(solution)/shard_map/pallas_call | solution.py:596
  31.0 2.0 %copy.8 = f32[2,256,1,512]{3,2,1,0:T(1,128)} copy(f32[2,256,1,512]{3,1,0,2:T(8,128)S(1)} %bitcast.6) | data formatting | bytes 2097152 | tf_op jit(solution)/shard_map/reshape | solution.py:634
  (2 shorter events, 0.0 us)
Async XLA Ops:
  0.0 3.0 %copy-start.1 = (s32[256,8]{1,0:T(8,128)S(1)}, s32[256,8]{1,0:T(8,128)}, u32[]{:S(2)}) copy-start(s32[256,8]{1,0:T(8,128)} %constant.4.clone.tab_ref) | copy-start | bytes 24580
  0.0 3.0 %copy-start.4 = (f32[2]{0:T(128)S(1)}, f32[2]{0:T(128)}, u32[]{:S(2)}) copy-start(f32[2]{0:T(128)} %rx_ref.1) | copy-start | bytes 28
  0.0 3.0 %copy-start.3 = (f32[2]{0:T(128)S(1)}, f32[2]{0:T(128)}, u32[]{:S(2)}) copy-start(f32[2]{0:T(128)} %th_ref.1) | copy-start | bytes 28
  0.0 3.0 %copy-start.2 = (s32[8,8]{1,0:T(8,128)S(1)}, s32[8,8]{1,0:T(8,128)}, u32[]{:S(2)}) copy-start(s32[8,8]{1,0:T(8,128)} %kind_ref.1) | copy-start | bytes 772
  0.0 3.0 %copy-start = (bf16[2,30,120,120]{3,2,1,0:T(8,128)(2,1)S(1)}, bf16[2,30,120,120]{3,2,1,0:T(8,128)(2,1)}, u32[]{:S(2)}) copy-start(bf16[2,30,120,120]{3,2,1,0:T(8,128)(2,1)} %k_in.1) | copy-start | bytes 5184004
where the time goes:
time: 33.2 us; the launch traced here: 33 us
  Pallas kernels  28 us (84%)
  local copies, waits for them, and re-layouts  4.99 us (15%)
    pallas_call x1, Pallas kernels, per_device(): pl.pallas_call(functools.partial(kernel, space_count), out_shape=jax.Shap...  28 us
    reshape x1, local copies, waits for them, and re-layouts, per_device(): return result.reshape(own, rows, layers, cells)  2.05 us
    unnamed x11, local copies, waits for them, and re-layouts  1.31 us
    another operation x2, local copies, waits for them, and re-layouts, per_device(): maps = jnp.stack([ordered, by_block])  0.89 us
    reshape x1, local copies, waits for them, and re-layouts, per_device(): low_map.reshape(SPLIT, out_rows)  0.74 us

commit v1 on v0

--- a/solution.py
+++ b/solution.py
@@ -65,13 +65,19 @@
     space_count,
     f_in,
     k_in,
+    tab_in,
+    map_in,
+    kind_in,
+    th_in,
+    rx_in,
+    result,
+    f_ref,
+    out_ref,
     tab_ref,
     lm_ref,
     kind_ref,
     th_ref,
     rx_ref,
-    out_ref,
-    f_ref,
     kraw,
     k2,
     low_send,
@@ -88,6 +94,7 @@
     ab_send,
     ab_recv,
     copy_sem,
+    small_sem,
     s1,
     r1,
     s2,
@@ -103,11 +110,6 @@
     m = lax.axis_index("mode")
     sx = lax.axis_index("space")
 
-    copy_f = pltpu.make_async_copy(f_in, f_ref, copy_sem.at[0])
-    copy_k = pltpu.make_async_copy(k_in, kraw, copy_sem.at[1])
-    copy_f.start()
-    copy_k.start()
-
     barrier = pltpu.get_barrier_semaphore()
     for step in range(1, SPLIT * SPLIT):
         other = lax.rem(q * SPLIT + m + step, SPLIT * SPLIT)
@@ -126,15 +128,37 @@
     def _():
         pl.semaphore_signal(barrier, inc=1, device_id={"space": sx + 1}, device_id_type=MESH)
 
-    copy_f.wait()
+    columns_in = [
+        pltpu.make_async_copy(
+            f_in.at[slot, :, 0, pl.ds(part * LANES, LANES)],
+            f_ref.at[part, slot],
+            copy_sem.at[part, slot],
+        )
+        for part in range(SPLIT)
+        for slot in range(OWN)
+    ]
+    small = [
+        pltpu.make_async_copy(tab_in, tab_ref, small_sem.at[0]),
+        pltpu.make_async_copy(map_in, lm_ref, small_sem.at[1]),
+        pltpu.make_async_copy(kind_in, kind_ref, small_sem.at[2]),
+        pltpu.make_async_copy(th_in, th_ref, small_sem.at[3]),
+        pltpu.make_async_copy(rx_in, rx_ref, small_sem.at[4]),
+    ]
+    copy_k = pltpu.make_async_copy(k_in, kraw, small_sem.at[5])
+    for item in columns_in + small + [copy_k]:
+        item.start()
+    for item in small + columns_in:
+        item.wait()
+
+    def load(slot, rows):
+        return jnp.concatenate([f_ref[part, slot, rows, :] for part in range(SPLIT)], axis=1)
 
     def extract(first, count):
         rows = lax.broadcasted_iota(jnp.int32, (count, OWN * ROWS), 1)
         chosen = jnp.where(tab_ref[first : first + count, 0:1] == rows, 1.0, 0.0).astype(BF16)
-        field = f_ref[...].reshape(OWN * ROWS, SPLIT * LANES).astype(BF16)
-        packed = dot(chosen, field).astype(BF16)
         for part in range(SPLIT):
-            low_send[part, first : first + count, :] = packed[:, part * LANES : (part + 1) * LANES]
+            field = f_ref[part].reshape(OWN * ROWS, LANES).astype(BF16)
+            low_send[part, first : first + count, :] = dot(chosen, field).astype(BF16)
 
     @pl.when(m == 0)
     def _():
@@ -145,8 +169,8 @@
         extract(HEAD, PACK - HEAD)
 
     for slot in range(OWN):
-        halo_send[0, slot] = f_ref[slot, 0:64, :].astype(BF16)
-        halo_send[1, slot] = f_ref[slot, ROWS - 64 : ROWS, :].astype(BF16)
+        halo_send[0, slot] = load(slot, slice(0, 64)).astype(BF16)
+        halo_send[1, slot] = load(slot, slice(ROWS - 64, ROWS)).astype(BF16)
 
     inner = (sx > 0) & (sx < space_count - 1)
     peers = SPLIT * SPLIT - 1
@@ -231,11 +255,25 @@
 
     lax.fori_loop(0, PAD_N, lay, 0)
 
+    lanes = lax.broadcasted_iota(jnp.int32, (8, PAD_J), 1)
+    low_count = kraw.shape[2]
+    block_rows = kraw.shape[1]
+    ordered = jnp.concatenate(
+        [lm_ref[...], jnp.full((1, PAD_J - low_count), -2, jnp.int32)], axis=1
+    )
+    ordered = jnp.broadcast_to(ordered, (8, PAD_J))
+    by_block = jnp.full((8, PAD_J), -2, jnp.int32)
+    for block in range(SPLIT):
+        moved = ordered
+        if block > 0:
+            moved = pltpu.roll(ordered, block * (PAD_N - block_rows), 1)
+        inside = (lanes >= block * PAD_N) & (lanes < block * PAD_N + block_rows)
+        by_block = jnp.where(inside, moved, by_block)
     for slot in range(OWN):
-        same = tab_ref[:, 1 + slot : 2 + slot] == lm_ref[0:1, :]
+        same = tab_ref[:, 1 + slot : 2 + slot] == ordered[0:1, :]
         pick[slot] = jnp.where(same, 1.0, 0.0).T.astype(BF16)
     mode_of = lax.broadcasted_iota(jnp.int32, (ROWS, PAD_J), 0) + m * ROWS
-    spread[...] = jnp.where(mode_of == lm_ref[1:2, :], 1.0, 0.0).astype(BF16)
+    spread[...] = jnp.where(mode_of == by_block[0:1, :], 1.0, 0.0).astype(BF16)
 
     def piece_wait(source, count, sender):
         pltpu.make_async_remote_copy(
@@ -298,7 +336,7 @@
         scale = nu_step * th_ref[slot]
         relax = dt_step * rx_ref[slot]
         blocks = [
-            f_ref[slot, pl.ds(pl.multiple_of(a * 64 + b * NVZ, NVZ), NVZ), :] for b in range(NVY)
+            load(slot, pl.ds(pl.multiple_of(a * 64 + b * NVZ, NVZ), NVZ)) for b in range(NVY)
         ]
         for b in range(NVY):
             here = blocks[b]
@@ -325,9 +363,10 @@
             )
             total = degree_c + (b + a + m * PER_VX)
             lost = jnp.where(total > DEG, relax, 0.0)
-            out_ref[slot, pl.ds(pl.multiple_of(a * 64 + b * NVZ, NVZ), NVZ), :] = (
-                here - scale * (y_term + z_term + bound_x * here) - lost * here
-            )
+            value = here - scale * (y_term + z_term + bound_x * here) - lost * here
+            rows = pl.ds(pl.multiple_of(a * 64 + b * NVZ, NVZ), NVZ)
+            for part in range(SPLIT):
+                out_ref[part, slot, rows, :] = value[:, part * LANES : (part + 1) * LANES]
         return carry
 
     lax.fori_loop(0, OWN * PER_VX, own_terms, 0)
@@ -340,13 +379,13 @@
         def part(i, carry):
             slot = i // 4
             r = lax.rem(i, 4) * 16
-            here = f_ref[slot, pl.ds(pl.multiple_of(a * 64 + r, 16), 16), :]
+            here = load(slot, pl.ds(pl.multiple_of(a * 64 + r, 16), 16))
             if a < PER_VX - 1:
-                above = f_ref[slot, pl.ds(pl.multiple_of((a + 1) * 64 + r, 16), 16), :]
+                above = load(slot, pl.ds(pl.multiple_of((a + 1) * 64 + r, 16), 16))
             else:
                 above = halo_recv[1, slot, pl.ds(pl.multiple_of(r, 16), 16), :].astype(F32)
             if a > 0:
-                below = f_ref[slot, pl.ds(pl.multiple_of((a - 1) * 64 + r, 16), 16), :]
+                below = load(slot, pl.ds(pl.multiple_of((a - 1) * 64 + r, 16), 16))
             else:
                 below = halo_recv[0, slot, pl.ds(pl.multiple_of(r, 16), 16), :].astype(F32)
             flux = root_up * above + root * below
@@ -502,10 +541,27 @@
             rows = pl.ds(pl.multiple_of(slot * 64 + r, 16), 16)
             here = pl.ds(pl.multiple_of(a * 64 + r, 16), 16)
             term = ab_recv[0, a, rows, :].astype(F32) + ab_recv[1, a, rows, :].astype(F32)
-            out_ref[slot, here, :] = out_ref[slot, here, :] - (nu_step * th_ref[slot]) * term
+            term = (nu_step * th_ref[slot]) * term
+            for part in range(SPLIT):
+                out_ref[part, slot, here, :] = (
+                    out_ref[part, slot, here, :] - term[:, part * LANES : (part + 1) * LANES]
+                )
             return carry
 
         lax.fori_loop(0, OWN * 4, add_x, 0)
+
+    def column_out(part, slot):
+        return pltpu.make_async_copy(
+            out_ref.at[part, slot],
+            result.at[slot, :, 0, pl.ds(pl.multiple_of(part * LANES, LANES), LANES)],
+            copy_sem.at[part, slot],
+        )
+
+    @pl.when(m >= 2)
+    def _():
+        for part in range(SPLIT):
+            for slot in range(OWN):
+                column_out(part, slot).start()
 
     @pl.when(m < 2)
     def _():
@@ -527,10 +583,10 @@
                     take()
                 else:
                     pl.when(m != sender)(take)
-            columns = pl.ds(pl.multiple_of(source * LANES, LANES), LANES)
             for slot in range(OWN):
                 gained = dot(spread[...], grecv[source, :, slot * LANES : (slot + 1) * LANES])
-                out_ref[slot, :, columns] = out_ref[slot, :, columns] + dt_step * gained
+                out_ref[source, slot] = out_ref[source, slot] + dt_step * gained
+                column_out(source, slot).start()
 
     @pl.when(m == 0)
     def _():
@@ -576,30 +632,32 @@
                 def _():
                     give(pair, target).wait_send()
 
+    for part in range(SPLIT):
+        for slot in range(OWN):
+            column_out(part, slot).wait()
+
 
 def per_device(space_count, distribution, kernels, pair_kind, low_map, thermal_speed, relax_rate):
     own, rows, layers, cells = distribution.shape
     assert (own, rows, layers, cells) == (OWN, ROWS, 1, SPLIT * LANES)
-    kinds, out_rows, low_count, _ = kernels.shape
-    field = distribution.reshape(own, rows, cells)
-    ordered = jnp.pad(low_map, (0, PAD_J - low_count), constant_values=-2)
-    by_block = jnp.pad(
-        low_map.reshape(SPLIT, out_rows), ((0, 0), (0, PAD_N - out_rows)), constant_values=-2
-    ).reshape(PAD_J)
-    maps = jnp.stack([ordered, by_block])
+    kinds, _, low_count, _ = kernels.shape
     table = jnp.asarray(packed_table())
-    vmem = pl.BlockSpec(memory_space=pltpu.VMEM)
-    smem = pl.BlockSpec(memory_space=pltpu.SMEM)
     anywhere = pl.BlockSpec(memory_space=pl.ANY)
     dma = pltpu.SemaphoreType.DMA
     ab_type = F32
     result = pl.pallas_call(
         functools.partial(kernel, space_count),
-        out_shape=jax.ShapeDtypeStruct((own, rows, cells), F32),
-        in_specs=[anywhere, anywhere, vmem, vmem, smem, smem, smem],
-        out_specs=vmem,
+        out_shape=jax.ShapeDtypeStruct(distribution.shape, F32),
+        in_specs=[anywhere] * 7,
+        out_specs=anywhere,
         scratch_shapes=[
-            pltpu.VMEM((own, rows, cells), F32),
+            pltpu.VMEM((SPLIT, own, rows, LANES), F32),
+            pltpu.VMEM((SPLIT, own, rows, LANES), F32),
+            pltpu.VMEM(table.shape, jnp.int32),
+            pltpu.VMEM((1, low_count), jnp.int32),
+            pltpu.SMEM(pair_kind.shape, jnp.int32),
+            pltpu.SMEM(thermal_speed.shape, F32),
+            pltpu.SMEM(relax_rate.shape, F32),
             pltpu.VMEM(kernels.shape, BF16),
             pltpu.VMEM((PAD_N, PAD_J, kinds * PAD_J), BF16),
             pltpu.VMEM((SPLIT, PACK, LANES), BF16),
@@ -615,7 +673,8 @@
             pltpu.VMEM((2, own, 64, cells), BF16),
             pltpu.VMEM((2, PER_VX, own * 64, cells), ab_type),
             pltpu.VMEM((2, PER_VX, own * 64, cells), ab_type),
-            dma((2,)),
+            dma((SPLIT, OWN)),
+            dma((6,)),
             dma((SPLIT, SPLIT)),
             dma((SPLIT, 2)),
             dma((SPLIT, SPLIT)),
@@ -628,10 +687,18 @@
             dma((2, PER_VX)),
         ],
         compiler_params=pltpu.CompilerParams(
-            collective_id=0, has_side_effects=True, vmem_limit_bytes=48 * 1024 * 1024
+            collective_id=0, has_side_effects=True, vmem_limit_bytes=60 * 1024 * 1024
         ),
-    )(field, kernels, table, maps, pair_kind, thermal_speed, relax_rate)
-    return result.reshape(own, rows, layers, cells)
+    )(
+        distribution,
+        kernels,
+        table,
+        low_map.reshape(1, low_count),
+        pair_kind,
+        thermal_speed,
+        relax_rate,
+    )
+    return result
 
 
 def solution(mesh):

time: 33.2 us -> 30.9 us (0.931)
  local copies, waits for them, and re-layouts: 4.99 us -> 2.91 us
    reshape x2 -> x0, local copies, waits for them, and re-layouts: 2.78 us -> none  [the longest x1 2.05 us: per_device(): return result.reshape(own, rows, layers, cells)]
    unnamed x11 -> x1, local copies, waits for them, and re-layouts: 1.31 us -> 2.91 us
    another operation x2 -> x0, local copies, waits for them, and re-layouts: 0.89 us -> none  [per_device(): maps = jnp.stack([ordered, by_block])]
where the time goes in v1:
time: 30.9 us; the launch traced here: 30.7 us
  Pallas kernels  27.8 us (90%)
  local copies, waits for them, and re-layouts  2.91 us (9%)
    pallas_call x1, Pallas kernels, per_device(): pl.pallas_call(functools.partial(kernel, space_count), out_shape=jax.Shap...  27.8 us
    unnamed x1, local copies, waits for them, and re-layouts  2.91 us

profile of v1, /device:TPU:0, one launch (start us, length us, event | category | flops | bytes accessed | tf_op | source)
XLA Modules:
  0.0 30.7 jit_solution(14839609208251931752)
XLA Ops:
  0.0 27.8 %shard_map.73 = f32[2,256,1,512]{3,2,1,0:T(1,128)} custom-call(f32[2,256,1,512]{3,2,1,0:T(1,128)} %f_in.1, bf16[2,30,120,120]{3,2,1,0:T(8,128)(2,1)} %k_in.1, s32[256,8]{1,0:T(8,128)} %constant.2.clone.tab_in, s32[1,120]{1,0:T(1,128)} %bitcast.1, s32[8,8]{1,0:T(8,128)} %kind_in.1, f32[2]{0:T(128)} %th_in.1, f32[2]{0:T(128)} %rx_in.1), custom_call_target="tpu_custom_call" | custom-call | tf_op jit(solution)/shard_map/pallas_call | solution.py:648
  27.8 2.9 %copy.9 = f32[2,256,1,512]{3,2,1,0:T(1,128)} copy(f32[2,256,1,512]{3,2,1,0:T(1,128)} %shard_map.73) | data formatting | bytes 2097152

commit v2 on v1

--- a/solution.py
+++ b/solution.py
@@ -85,6 +85,7 @@
     low,
     pmat,
     gsum,
+    total,
     gsend,
     grecv,
     pick,
@@ -110,24 +111,6 @@
     m = lax.axis_index("mode")
     sx = lax.axis_index("space")
 
-    barrier = pltpu.get_barrier_semaphore()
-    for step in range(1, SPLIT * SPLIT):
-        other = lax.rem(q * SPLIT + m + step, SPLIT * SPLIT)
-        pl.semaphore_signal(
-            barrier,
-            inc=1,
-            device_id={"species": other // SPLIT, "mode": lax.rem(other, SPLIT)},
-            device_id_type=MESH,
-        )
-
-    @pl.when(sx > 0)
-    def _():
-        pl.semaphore_signal(barrier, inc=1, device_id={"space": sx - 1}, device_id_type=MESH)
-
-    @pl.when(sx < space_count - 1)
-    def _():
-        pl.semaphore_signal(barrier, inc=1, device_id={"space": sx + 1}, device_id_type=MESH)
-
     columns_in = [
         pltpu.make_async_copy(
             f_in.at[slot, :, 0, pl.ds(part * LANES, LANES)],
@@ -145,9 +128,30 @@
         pltpu.make_async_copy(rx_in, rx_ref, small_sem.at[4]),
     ]
     copy_k = pltpu.make_async_copy(k_in, kraw, small_sem.at[5])
-    for item in columns_in + small + [copy_k]:
+    for item in columns_in + small[:1]:
         item.start()
-    for item in small + columns_in:
+
+    barrier = pltpu.get_barrier_semaphore()
+    for step in range(1, SPLIT * SPLIT):
+        other = lax.rem(q * SPLIT + m + step, SPLIT * SPLIT)
+        pl.semaphore_signal(
+            barrier,
+            inc=1,
+            device_id={"species": other // SPLIT, "mode": lax.rem(other, SPLIT)},
+            device_id_type=MESH,
+        )
+
+    @pl.when(sx > 0)
+    def _():
+        pl.semaphore_signal(barrier, inc=1, device_id={"space": sx - 1}, device_id_type=MESH)
+
+    @pl.when(sx < space_count - 1)
+    def _():
+        pl.semaphore_signal(barrier, inc=1, device_id={"space": sx + 1}, device_id_type=MESH)
+
+    for item in small[1:] + [copy_k]:
+        item.start()
+    for item in columns_in + small[:1]:
         item.wait()
 
     def load(slot, rows):
@@ -167,10 +171,6 @@
     @pl.when(m == 1)
     def _():
         extract(HEAD, PACK - HEAD)
-
-    for slot in range(OWN):
-        halo_send[0, slot] = load(slot, slice(0, 64)).astype(BF16)
-        halo_send[1, slot] = load(slot, slice(ROWS - 64, ROWS)).astype(BF16)
 
     inner = (sx > 0) & (sx < space_count - 1)
     peers = SPLIT * SPLIT - 1
@@ -220,6 +220,10 @@
         for step in (1, 2, 3, 0):
             tail_copies(step).start()
 
+    for slot in range(OWN):
+        halo_send[0, slot] = load(slot, slice(0, 64)).astype(BF16)
+        halo_send[1, slot] = load(slot, slice(ROWS - 64, ROWS)).astype(BF16)
+
     def halo(way):
         return pltpu.make_async_remote_copy(
             src_ref=halo_send.at[way],
@@ -230,7 +234,7 @@
             device_id_type=MESH,
         )
 
-    @pl.when(m >= 2)
+    @pl.when((m == 1) | (m == 3))
     def _():
         halo(0).start()
 
@@ -238,7 +242,8 @@
     def _():
         halo(1).start()
 
-    copy_k.wait()
+    for item in small[1:] + [copy_k]:
+        item.wait()
 
     def lay(n, carry):
         k2[n] = jnp.zeros((PAD_J, NKIND * PAD_J), BF16)
@@ -271,7 +276,7 @@
         by_block = jnp.where(inside, moved, by_block)
     for slot in range(OWN):
         same = tab_ref[:, 1 + slot : 2 + slot] == ordered[0:1, :]
-        pick[slot] = jnp.where(same, 1.0, 0.0).T.astype(BF16)
+        pick[slot * PAD_J : (slot + 1) * PAD_J, :] = jnp.where(same, 1.0, 0.0).T.astype(BF16)
     mode_of = lax.broadcasted_iota(jnp.int32, (ROWS, PAD_J), 0) + m * ROWS
     spread[...] = jnp.where(mode_of == by_block[0:1, :], 1.0, 0.0).astype(BF16)
 
@@ -321,7 +326,7 @@
     def _():
         halo(1).start()
 
-    @pl.when(m == 1)
+    @pl.when(m == 2)
     def _():
         halo(0).start()
 
@@ -442,27 +447,32 @@
         source = lax.rem(q + SPLIT - back, SPLIT)
         for step in range(1, SPLIT):
             forward_wait(source, step)
-        packed = full[source]
+        picked = dot(pick[...], full[source])
         for slot in range(OWN):
-            low[source, :, slot * LANES : (slot + 1) * LANES] = dot(pick[slot], packed)
-
-    def partners(pair, carry):
+            low[source, :, slot * LANES : (slot + 1) * LANES] = picked[
+                slot * PAD_J : (slot + 1) * PAD_J
+            ]
+
+    def of_species(r):
+        return low[r // OWN, :, (r % OWN) * LANES : (r % OWN + 1) * LANES]
+
+    everyone = of_species(0)
+    for r in range(1, SPLIT * OWN):
+        everyone = everyone + of_species(r)
+    total[...] = everyone
+
+    def partners(pair):
+        def one(slot):
+            first = jnp.zeros((PAD_J, LANES), F32)
+            for r in range(SPLIT * OWN):
+                weight = jnp.where(kind_ref[pair * OWN + slot, r] == 0, 1.0, 0.0)
+                first = first + weight * of_species(r)
+            cut = slice(slot * LANES, (slot + 1) * LANES)
+            pmat[pair, 0:PAD_J, cut] = first.astype(BF16)
+            pmat[pair, PAD_J:, cut] = (total[...] - first).astype(BF16)
+
         for slot in range(OWN):
-            sums = [jnp.zeros((PAD_J, LANES), F32) for _ in range(NKIND)]
-            for r in range(SPLIT * OWN):
-                values = low[r // OWN, :, (r % OWN) * LANES : (r % OWN + 1) * LANES]
-                kind_here = kind_ref[pair * OWN + slot, r]
-                for kind in range(NKIND):
-                    sums[kind] = sums[kind] + jnp.where(kind_here == kind, 1.0, 0.0) * values
-            for kind in range(NKIND):
-                pmat[
-                    pair,
-                    kind * PAD_J : (kind + 1) * PAD_J,
-                    slot * LANES : (slot + 1) * LANES,
-                ] = sums[kind].astype(BF16)
-        return carry
-
-    lax.fori_loop(0, SPLIT, partners, 0)
+            one(slot)
 
     def give(pair, target):
         return pltpu.make_async_remote_copy(
@@ -491,6 +501,7 @@
 
     for step in (1, 2, 3, 0):
         pair = lax.rem(q + step, SPLIT)
+        partners(pair)
         collide(pair)
         for target in range(2):
             if step > 0:
@@ -583,9 +594,11 @@
                     take()
                 else:
                     pl.when(m != sender)(take)
+            gained = dot(spread[...], grecv[source])
             for slot in range(OWN):
-                gained = dot(spread[...], grecv[source, :, slot * LANES : (slot + 1) * LANES])
-                out_ref[source, slot] = out_ref[source, slot] + dt_step * gained
+                out_ref[source, slot] = (
+                    out_ref[source, slot] + dt_step * gained[:, slot * LANES : (slot + 1) * LANES]
+                )
                 column_out(source, slot).start()
 
     @pl.when(m == 0)
@@ -635,6 +648,23 @@
     for part in range(SPLIT):
         for slot in range(OWN):
             column_out(part, slot).wait()
+
+
+def write_out(source, result, sems):
+    count = sems.shape[0]
+    rows = result.shape[1] // count
+    copies = [
+        pltpu.make_async_copy(
+            source.at[:, pl.ds(piece * rows, rows)],
+            result.at[:, pl.ds(piece * rows, rows)],
+            sems.at[piece],
+        )
+        for piece in range(count)
+    ]
+    for item in copies:
+        item.start()
+    for item in copies:
+        item.wait()
 
 
 def per_device(space_count, distribution, kernels, pair_kind, low_map, thermal_speed, relax_rate):
@@ -645,7 +675,7 @@
     anywhere = pl.BlockSpec(memory_space=pl.ANY)
     dma = pltpu.SemaphoreType.DMA
     ab_type = F32
-    result = pl.pallas_call(
+    stepped = pl.pallas_call(
         functools.partial(kernel, space_count),
         out_shape=jax.ShapeDtypeStruct(distribution.shape, F32),
         in_specs=[anywhere] * 7,
@@ -665,9 +695,10 @@
             pltpu.VMEM((SPLIT, PAD_J, own * LANES), F32),
             pltpu.VMEM((SPLIT, kinds * PAD_J, own * LANES), BF16),
             pltpu.VMEM((PAD_N, own * LANES), F32),
+            pltpu.VMEM((PAD_J, LANES), F32),
             pltpu.VMEM((SPLIT, PAD_N, own * LANES), BF16),
             pltpu.VMEM((SPLIT, SPLIT * PAD_N, own * LANES), BF16),
-            pltpu.VMEM((own, PAD_J, PACK), BF16),
+            pltpu.VMEM((own * PAD_J, PACK), BF16),
             pltpu.VMEM((ROWS, PAD_J), BF16),
             pltpu.VMEM((2, own, 64, cells), BF16),
             pltpu.VMEM((2, own, 64, cells), BF16),
@@ -698,7 +729,14 @@
         thermal_speed,
         relax_rate,
     )
-    return result
+    return pl.pallas_call(
+        write_out,
+        out_shape=jax.ShapeDtypeStruct(distribution.shape, F32),
+        in_specs=[anywhere],
+        out_specs=anywhere,
+        scratch_shapes=[dma((8,))],
+        compiler_params=pltpu.CompilerParams(vmem_limit_bytes=60 * 1024 * 1024),
+    )(stepped)
 
 
 def solution(mesh):

time: 30.9 us -> 60.4 us (1.95)
  Pallas kernels: 27.8 us -> 60.2 us
  local copies, waits for them, and re-layouts: 2.91 us -> 0 us
    pallas_call x0 -> x1, Pallas kernels: none -> 32.9 us  [per_device(): pl.pallas_call(write_out, out_shape=jax.ShapeDtypeStruct(distribution.sha...]
    unnamed x1 -> x0, local copies, waits for them, and re-layouts: 2.91 us -> none
where the time goes in v2:
time: 60.4 us; the launch traced here: 60.2 us
  Pallas kernels  60.2 us (100%)
    pallas_call x1, Pallas kernels, per_device(): pl.pallas_call(write_out, out_shape=jax.ShapeDtypeStruct(distribution.sha...  32.9 us
    pallas_call x1, Pallas kernels, per_device(): pl.pallas_call(functools.partial(kernel, space_count), out_shape=jax.Shap...  27.3 us

profile of v2, /device:TPU:0, one launch (start us, length us, event | category | flops | bytes accessed | tf_op | source)
XLA Modules:
  0.0 60.2 jit_solution(14911215159085611573)
XLA Ops:
  0.0 27.3 %shard_map.73.source = f32[2,256,1,512]{3,2,1,0:T(1,128)} custom-call(f32[2,256,1,512]{3,2,1,0:T(1,128)} %f_in.1, bf16[2,30,120,120]{3,2,1,0:T(8,128)(2,1)} %k_in.1, s32[256,8]{1,0:T(8,128)} %constant.2.clone.tab_in, s32[1,120]{1,0:T(1,128)} %bitcast.1, s32[8,8]{1,0:T(8,128)} %kind_in.1, f32[2]{0:T(128)} %th_in.1, f32[2]{0:T(128)} %rx_in.1), custom_call_target="tpu_custom_call" | custom-call | tf_op jit(solution)/shard_map/pallas_call | solution.py:678
  27.3 32.9 %shard_map.74 = f32[2,256,1,512]{3,2,1,0:T(1,128)} custom-call(f32[2,256,1,512]{3,2,1,0:T(1,128)} %shard_map.73.source), custom_call_target="tpu_custom_call" | custom-call | tf_op jit(solution)/shard_map/pallas_call | solution.py:732

commit v3 on v2

--- a/solution.py
+++ b/solution.py
@@ -92,6 +92,7 @@
     spread,
     halo_send,
     halo_recv,
+    edge_recv,
     ab_send,
     ab_recv,
     copy_sem,
@@ -106,6 +107,8 @@
     hr,
     xs,
     xr,
+    es,
+    er,
 ):
     q = lax.axis_index("species")
     m = lax.axis_index("mode")
@@ -376,24 +379,24 @@
 
     lax.fori_loop(0, OWN * PER_VX, own_terms, 0)
 
+    def degree_roots(a):
+        degree = (m * PER_VX + a).astype(F32)
+        below = jnp.sqrt(jnp.full((8, 128), degree, F32))[0:1, 0:1]
+        above = jnp.sqrt(jnp.full((8, 128), degree + 1.0, F32))[0:1, 0:1]
+        return below, above
+
     def x_parts(a):
-        degree = (m * PER_VX + a).astype(F32)
-        root = jnp.sqrt(jnp.full((8, 128), degree, F32))[0:1, 0:1]
-        root_up = jnp.sqrt(jnp.full((8, 128), degree + 1.0, F32))[0:1, 0:1]
+        root, root_up = degree_roots(a)
 
         def part(i, carry):
             slot = i // 4
             r = lax.rem(i, 4) * 16
             here = load(slot, pl.ds(pl.multiple_of(a * 64 + r, 16), 16))
+            flux = jnp.zeros_like(here)
             if a < PER_VX - 1:
-                above = load(slot, pl.ds(pl.multiple_of((a + 1) * 64 + r, 16), 16))
-            else:
-                above = halo_recv[1, slot, pl.ds(pl.multiple_of(r, 16), 16), :].astype(F32)
+                flux = flux + root_up * load(slot, pl.ds(pl.multiple_of((a + 1) * 64 + r, 16), 16))
             if a > 0:
-                below = load(slot, pl.ds(pl.multiple_of((a - 1) * 64 + r, 16), 16))
-            else:
-                below = halo_recv[0, slot, pl.ds(pl.multiple_of(r, 16), 16), :].astype(F32)
-            flux = root_up * above + root * below
+                flux = flux + root * load(slot, pl.ds(pl.multiple_of((a - 1) * 64 + r, 16), 16))
             rows = pl.ds(pl.multiple_of(slot * 64 + r, 16), 16)
             ab_send[0, a, rows, :] = (0.5 * flux - 0.5 * bound_x * here).astype(ab_send.dtype)
             ab_send[1, a, rows, :] = (-0.5 * flux - 0.5 * bound_x * here).astype(ab_send.dtype)
@@ -423,12 +426,14 @@
     @pl.when(sx == space_count - 1)
     def _():
         ab_recv[0] = jnp.zeros(ab_recv.shape[1:], ab_recv.dtype)
+        edge_recv[0] = jnp.zeros(edge_recv.shape[1:], BF16)
 
     @pl.when(sx == 0)
     def _():
         ab_recv[1] = jnp.zeros(ab_recv.shape[1:], ab_recv.dtype)
-
-    for a in (1, 2):
+        edge_recv[1] = jnp.zeros(edge_recv.shape[1:], BF16)
+
+    for a in range(PER_VX):
         x_parts(a)
         send_layers(a)
 
@@ -532,11 +537,25 @@
     def _():
         halo_recv[1] = jnp.zeros(halo_recv.shape[1:], BF16)
 
-    for a in (0, 3):
-        x_parts(a)
-        send_layers(a)
-
-    for a in (1, 2, 0, 3):
+    def edges(way):
+        return pltpu.make_async_remote_copy(
+            src_ref=halo_recv,
+            dst_ref=edge_recv.at[way],
+            send_sem=es.at[way],
+            recv_sem=er.at[way],
+            device_id={"space": sx - 1 if way == 0 else sx + 1},
+            device_id_type=MESH,
+        )
+
+    @pl.when(sx > 0)
+    def _():
+        edges(0).start()
+
+    @pl.when(sx < space_count - 1)
+    def _():
+        edges(1).start()
+
+    for a in range(PER_VX):
 
         @pl.when(sx < space_count - 1)
         def _():
@@ -546,12 +565,28 @@
         def _():
             layer(1, a).wait_recv()
 
+    @pl.when(sx < space_count - 1)
+    def _():
+        edges(0).wait_recv()
+
+    @pl.when(sx > 0)
+    def _():
+        edges(1).wait_recv()
+
+    for a in range(PER_VX):
+        root, root_up = degree_roots(a)
+
         def add_x(i, carry):
             slot = i // 4
-            r = lax.rem(i, 4) * 16
+            r = pl.multiple_of(lax.rem(i, 4) * 16, 16)
             rows = pl.ds(pl.multiple_of(slot * 64 + r, 16), 16)
             here = pl.ds(pl.multiple_of(a * 64 + r, 16), 16)
-            term = ab_recv[0, a, rows, :].astype(F32) + ab_recv[1, a, rows, :].astype(F32)
+            term = ab_recv[0, a, rows, :] + ab_recv[1, a, rows, :]
+            side = {0: 0, PER_VX - 1: 1}.get(a)
+            if side is not None:
+                up = edge_recv[0, side, slot, pl.ds(r, 16), :].astype(F32)
+                down = edge_recv[1, side, slot, pl.ds(r, 16), :].astype(F32)
+                term = term + (0.5 * (root_up if side else root)) * (up - down)
             term = (nu_step * th_ref[slot]) * term
             for part in range(SPLIT):
                 out_ref[part, slot, here, :] = (
@@ -634,6 +669,14 @@
         def _():
             layer(1, a).wait_send()
 
+    @pl.when(sx > 0)
+    def _():
+        edges(0).wait_send()
+
+    @pl.when(sx < space_count - 1)
+    def _():
+        edges(1).wait_send()
+
     for step in range(SPLIT):
         pair = lax.rem(q + step, SPLIT)
         for target in range(2):
@@ -650,21 +693,21 @@
             column_out(part, slot).wait()
 
 
-def write_out(source, result, sems):
-    count = sems.shape[0]
+def write_out(source, result, held, sems):
+    count = sems.shape[1]
     rows = result.shape[1] // count
-    copies = [
-        pltpu.make_async_copy(
-            source.at[:, pl.ds(piece * rows, rows)],
-            result.at[:, pl.ds(piece * rows, rows)],
-            sems.at[piece],
-        )
-        for piece in range(count)
-    ]
-    for item in copies:
-        item.start()
-    for item in copies:
-        item.wait()
+
+    def move(src, dst, way, piece):
+        cut = pl.ds(piece * rows, rows)
+        return pltpu.make_async_copy(src.at[:, cut], dst.at[:, cut], sems.at[way, piece])
+
+    for piece in range(count):
+        move(source, held, 0, piece).start()
+    for piece in range(count):
+        move(source, held, 0, piece).wait()
+        move(held, result, 1, piece).start()
+    for piece in range(count):
+        move(held, result, 1, piece).wait()
 
 
 def per_device(space_count, distribution, kernels, pair_kind, low_map, thermal_speed, relax_rate):
@@ -702,6 +745,7 @@
             pltpu.VMEM((ROWS, PAD_J), BF16),
             pltpu.VMEM((2, own, 64, cells), BF16),
             pltpu.VMEM((2, own, 64, cells), BF16),
+            pltpu.VMEM((2, 2, own, 64, cells), BF16),
             pltpu.VMEM((2, PER_VX, own * 64, cells), ab_type),
             pltpu.VMEM((2, PER_VX, own * 64, cells), ab_type),
             dma((SPLIT, OWN)),
@@ -716,6 +760,8 @@
             dma((2,)),
             dma((2, PER_VX)),
             dma((2, PER_VX)),
+            dma((2,)),
+            dma((2,)),
         ],
         compiler_params=pltpu.CompilerParams(
             collective_id=0, has_side_effects=True, vmem_limit_bytes=60 * 1024 * 1024
@@ -734,7 +780,7 @@
         out_shape=jax.ShapeDtypeStruct(distribution.shape, F32),
         in_specs=[anywhere],
         out_specs=anywhere,
-        scratch_shapes=[dma((8,))],
+        scratch_shapes=[pltpu.VMEM(distribution.shape, F32), dma((2, 4))],
         compiler_params=pltpu.CompilerParams(vmem_limit_bytes=60 * 1024 * 1024),
     )(stepped)
 

time: 60.4 us -> 29.5 us (0.49)
  Pallas kernels: 60.2 us -> 29.3 us
    pallas_call x1, Pallas kernels: 32.9 us -> 1.98 us  [per_device(): pl.pallas_call(write_out, out_shape=jax.ShapeDtypeStruct(distribution.sha...]
where the time goes in v3:
time: 29.5 us; the launch traced here: 29.3 us
  Pallas kernels  29.3 us (99%)
    pallas_call x1, Pallas kernels, per_device(): pl.pallas_call(functools.partial(kernel, space_count), out_shape=jax.Shap...  27.3 us
    pallas_call x1, Pallas kernels, per_device(): pl.pallas_call(write_out, out_shape=jax.ShapeDtypeStruct(distribution.sha...  1.98 us

profile of v3, /device:TPU:0, one launch (start us, length us, event | category | flops | bytes accessed | tf_op | source)
XLA Modules:
  0.0 29.3 jit_solution(845186439189636267)
XLA Ops:
  0.0 27.3 %shard_map.73.source = f32[2,256,1,512]{3,2,1,0:T(1,128)} custom-call(f32[2,256,1,512]{3,2,1,0:T(1,128)} %f_in.1, bf16[2,30,120,120]{3,2,1,0:T(8,128)(2,1)} %k_in.1, s32[256,8]{1,0:T(8,128)} %constant.2.clone.tab_in, s32[1,120]{1,0:T(1,128)} %bitcast.1, s32[8,8]{1,0:T(8,128)} %kind_in.1, f32[2]{0:T(128)} %th_in.1, f32[2]{0:T(128)} %rx_in.1), custom_call_target="tpu_custom_call" | custom-call | tf_op jit(solution)/shard_map/pallas_call | solution.py:721
  27.3 2.0 %shard_map.74 = f32[2,256,1,512]{3,2,1,0:T(1,128)} custom-call(f32[2,256,1,512]{3,2,1,0:T(1,128)} %shard_map.73.source), custom_call_target="tpu_custom_call" | custom-call | tf_op jit(solution)/shard_map/pallas_call | solution.py:778

commit v4 on v3

--- a/solution.py
+++ b/solution.py
@@ -84,7 +84,6 @@
     full,
     low,
     pmat,
-    gsum,
     total,
     gsend,
     grecv,
@@ -304,7 +303,7 @@
             device_id_type=MESH,
         )
 
-    for back in range(SPLIT):
+    for back in (1, 2, 3, 0):
         source = lax.rem(q + SPLIT - back, SPLIT)
 
         if back > 0:
@@ -448,7 +447,7 @@
             device_id_type=MESH,
         ).wait_recv()
 
-    for back in range(SPLIT):
+    for back in (1, 2, 3, 0):
         source = lax.rem(q + SPLIT - back, SPLIT)
         for step in range(1, SPLIT):
             forward_wait(source, step)
@@ -489,20 +488,11 @@
             device_id_type=MESH,
         )
 
-    group = 8
-
     def collide(pair):
-        def some(i, carry):
-            left = k2[pl.ds(pl.multiple_of(i * group, group), group)]
-            product = dot(left.reshape(group * PAD_J, NKIND * PAD_J), pmat[pair])
-            own = low[pair]
-            gsum[pl.ds(pl.multiple_of(i * group, group), group), :] = jnp.sum(
-                product.reshape(group, PAD_J, OWN * LANES) * own[None], axis=1
-            )
-            return carry
-
-        lax.fori_loop(0, PAD_N // group, some, 0)
-        gsend[pair] = gsum[...].astype(BF16)
+        product = dot(k2[...].reshape(PAD_N * PAD_J, NKIND * PAD_J), pmat[pair])
+        own = low[pair]
+        gained = jnp.sum(product.reshape(PAD_N, PAD_J, OWN * LANES) * own[None], axis=1)
+        gsend[pair] = gained.astype(BF16)
 
     for step in (1, 2, 3, 0):
         pair = lax.rem(q + step, SPLIT)
@@ -611,7 +601,7 @@
 
     @pl.when(m < 2)
     def _():
-        for back in range(SPLIT):
+        for back in (1, 2, 3, 0):
             source = lax.rem(q + SPLIT - back, SPLIT)
             for sender in range(SPLIT):
 
@@ -737,7 +727,6 @@
             pltpu.VMEM((SPLIT, PACK, LANES), BF16),
             pltpu.VMEM((SPLIT, PAD_J, own * LANES), F32),
             pltpu.VMEM((SPLIT, kinds * PAD_J, own * LANES), BF16),
-            pltpu.VMEM((PAD_N, own * LANES), F32),
             pltpu.VMEM((PAD_J, LANES), F32),
             pltpu.VMEM((SPLIT, PAD_N, own * LANES), BF16),
             pltpu.VMEM((SPLIT, SPLIT * PAD_N, own * LANES), BF16),
@@ -780,7 +769,7 @@
         out_shape=jax.ShapeDtypeStruct(distribution.shape, F32),
         in_specs=[anywhere],
         out_specs=anywhere,
-        scratch_shapes=[pltpu.VMEM(distribution.shape, F32), dma((2, 4))],
+        scratch_shapes=[pltpu.VMEM(distribution.shape, F32), dma((2, 8))],
         compiler_params=pltpu.CompilerParams(vmem_limit_bytes=60 * 1024 * 1024),
     )(stepped)
 

time: 29.5 us -> 30.5 us (1.034)
  Pallas kernels: 29.3 us -> 30.4 us
    pallas_call x1, Pallas kernels: 27.3 us -> 28.3 us  [per_device(): pl.pallas_call(functools.partial(kernel, space_count), out_shape=jax.Shap...]
where the time goes in v4:
time: 30.5 us; the launch traced here: 30.4 us
  Pallas kernels  30.4 us (100%)
    pallas_call x1, Pallas kernels, per_device(): pl.pallas_call(functools.partial(kernel, space_count), out_shape=jax.Shap...  28.3 us
    pallas_call x1, Pallas kernels, per_device(): pl.pallas_call(write_out, out_shape=jax.ShapeDtypeStruct(distribution.sha...  2.09 us

profile of v4, /device:TPU:0, one launch (start us, length us, event | category | flops | bytes accessed | tf_op | source)
XLA Modules:
  0.0 30.4 jit_solution(5039471822936332081)
XLA Ops:
  0.0 28.3 %shard_map.73.source = f32[2,256,1,512]{3,2,1,0:T(1,128)} custom-call(f32[2,256,1,512]{3,2,1,0:T(1,128)} %f_in.1, bf16[2,30,120,120]{3,2,1,0:T(8,128)(2,1)} %k_in.1, s32[256,8]{1,0:T(8,128)} %constant.2.clone.tab_in, s32[1,120]{1,0:T(1,128)} %bitcast.1, s32[8,8]{1,0:T(8,128)} %kind_in.1, f32[2]{0:T(128)} %th_in.1, f32[2]{0:T(128)} %rx_in.1), custom_call_target="tpu_custom_call" | custom-call | tf_op jit(solution)/shard_map/pallas_call | solution.py:711
  28.3 2.1 %shard_map.74 = f32[2,256,1,512]{3,2,1,0:T(1,128)} custom-call(f32[2,256,1,512]{3,2,1,0:T(1,128)} %shard_map.73.source), custom_call_target="tpu_custom_call" | custom-call | tf_op jit(solution)/shard_map/pallas_call | solution.py:767

commit v5 on v3

--- a/solution.py
+++ b/solution.py
@@ -52,9 +52,14 @@
             for mode in held:
                 table[row, 0] = slot * ROWS + mode - first
                 table[row, 1 + slot] = mode
+                table[row, 3] = first // ROWS
                 row += 1
         assert row <= (HEAD if start == 0 else PACK)
     return table
+
+
+def each(count, body):
+    lax.fori_loop(0, count, lambda i, carry: (body(i), carry)[1], 0)
 
 
 def dot(left, right):
@@ -90,6 +95,7 @@
     grecv,
     pick,
     spread,
+    chooser,
     halo_send,
     halo_recv,
     edge_recv,
@@ -135,8 +141,8 @@
         item.start()
 
     barrier = pltpu.get_barrier_semaphore()
-    for step in range(1, SPLIT * SPLIT):
-        other = lax.rem(q * SPLIT + m + step, SPLIT * SPLIT)
+    def greet(step):
+        other = lax.rem(q * SPLIT + m + 1 + step, SPLIT * SPLIT)
         pl.semaphore_signal(
             barrier,
             inc=1,
@@ -144,6 +150,8 @@
             device_id_type=MESH,
         )
 
+    each(SPLIT * SPLIT - 1, greet)
+
     @pl.when(sx > 0)
     def _():
         pl.semaphore_signal(barrier, inc=1, device_id={"space": sx - 1}, device_id_type=MESH)
@@ -160,20 +168,17 @@
     def load(slot, rows):
         return jnp.concatenate([f_ref[part, slot, rows, :] for part in range(SPLIT)], axis=1)
 
-    def extract(first, count):
-        rows = lax.broadcasted_iota(jnp.int32, (count, OWN * ROWS), 1)
-        chosen = jnp.where(tab_ref[first : first + count, 0:1] == rows, 1.0, 0.0).astype(BF16)
-        for part in range(SPLIT):
+    @pl.when(m < 2)
+    def _():
+        rows = lax.broadcasted_iota(jnp.int32, (PACK, OWN * ROWS), 1)
+        chosen = (tab_ref[:, 0:1] == rows) & (tab_ref[:, 3:4] == m)
+        chooser[...] = jnp.where(chosen, 1.0, 0.0).astype(BF16)
+
+        def extract(part):
             field = f_ref[part].reshape(OWN * ROWS, LANES).astype(BF16)
-            low_send[part, first : first + count, :] = dot(chosen, field).astype(BF16)
-
-    @pl.when(m == 0)
-    def _():
-        extract(0, HEAD)
-
-    @pl.when(m == 1)
-    def _():
-        extract(HEAD, PACK - HEAD)
+            low_send[part] = dot(chooser[...], field).astype(BF16)
+
+        each(SPLIT, extract)
 
     inner = (sx > 0) & (sx < space_count - 1)
     peers = SPLIT * SPLIT - 1
@@ -198,34 +203,50 @@
 
     head_last = HEAD - 3 * PIECE
 
-    def head_copies(step):
-        part = lax.rem(q + step, SPLIT)
-        found = []
-        for piece in (3, 1, 2, 0):
-            if step == 0 and piece == 0:
-                continue
-            count = PIECE if piece < 3 else head_last
-            found.append(scatter(part, piece, piece * PIECE, count, 0))
-        return found
-
-    def tail_copies(step):
-        return scatter(lax.rem(q + step, SPLIT), 3, HEAD, PACK - HEAD, 1)
+    def head_copies(act):
+        def one(i):
+            part = lax.rem(q + 1 + i // 3, SPLIT)
+            piece = lax.rem(i, 3)
+
+            @pl.when((part != q) | (piece != 0))
+            def _():
+                act(scatter(part, piece, pl.multiple_of(piece * PIECE, PIECE), PIECE, 0))
+
+        each(SPLIT * 3, one)
+        each(
+            SPLIT,
+            lambda i: act(scatter(lax.rem(q + 1 + i, SPLIT), 3, 3 * PIECE, head_last, 0)),
+        )
+
+    def tail_copies(act):
+        each(
+            SPLIT,
+            lambda i: act(scatter(lax.rem(q + 1 + i, SPLIT), 3, HEAD, PACK - HEAD, 1)),
+        )
+
+    def start(item):
+        item.start()
+
+    def sent(item):
+        item.wait_send()
 
     @pl.when(m == 0)
     def _():
-        for step in (1, 2, 3, 0):
-            for item in head_copies(step):
-                item.start()
+        head_copies(start)
         full[q, 0:PIECE, :] = low_send[q, 0:PIECE, :]
 
     @pl.when(m == 1)
     def _():
-        for step in (1, 2, 3, 0):
-            tail_copies(step).start()
-
-    for slot in range(OWN):
-        halo_send[0, slot] = load(slot, slice(0, 64)).astype(BF16)
-        halo_send[1, slot] = load(slot, slice(ROWS - 64, ROWS)).astype(BF16)
+        tail_copies(start)
+
+    def narrow(i):
+        slot = i // 4
+        r = pl.multiple_of(lax.rem(i, 4) * 16, 16)
+        for way in range(2):
+            plane = load(slot, pl.ds(way * (ROWS - 64) + r, 16))
+            halo_send[way, slot, pl.ds(r, 16), :] = plane.astype(BF16)
+
+    each(OWN * 4, narrow)
 
     def halo(way):
         return pltpu.make_async_remote_copy(
@@ -304,16 +325,10 @@
             device_id_type=MESH,
         )
 
-    for back in range(SPLIT):
-        source = lax.rem(q + SPLIT - back, SPLIT)
-
-        if back > 0:
-
-            @pl.when(m == 0)
-            def _():
-                piece_wait(source, PIECE, 0)
-
-        @pl.when((m == 1) | (m == 2))
+    def pass_on(i):
+        source = lax.rem(q + 2 * SPLIT - 1 - i, SPLIT)
+
+        @pl.when((m < 3) & ((m > 0) | (source != q)))
         def _():
             piece_wait(source, PIECE, 0)
 
@@ -322,8 +337,9 @@
             piece_wait(source, head_last, 0)
             piece_wait(source, PACK - HEAD, 1)
 
-        for step in range(1, SPLIT):
-            forward(source, step).start()
+        each(SPLIT - 1, lambda step: forward(source, step + 1).start())
+
+    each(SPLIT, pass_on)
 
     @pl.when(m < 2)
     def _():
@@ -380,29 +396,29 @@
     lax.fori_loop(0, OWN * PER_VX, own_terms, 0)
 
     def degree_roots(a):
-        degree = (m * PER_VX + a).astype(F32)
+        degree = jnp.asarray(m * PER_VX + a, jnp.int32).astype(F32)
         below = jnp.sqrt(jnp.full((8, 128), degree, F32))[0:1, 0:1]
         above = jnp.sqrt(jnp.full((8, 128), degree + 1.0, F32))[0:1, 0:1]
         return below, above
 
     def x_parts(a):
         root, root_up = degree_roots(a)
-
-        def part(i, carry):
+        root_up = jnp.where(a < PER_VX - 1, root_up, 0.0)
+        root = jnp.where(a > 0, root, 0.0)
+        above = jnp.minimum(a + 1, PER_VX - 1) * 64
+        below = jnp.maximum(a - 1, 0) * 64
+
+        def part(i):
             slot = i // 4
             r = lax.rem(i, 4) * 16
             here = load(slot, pl.ds(pl.multiple_of(a * 64 + r, 16), 16))
-            flux = jnp.zeros_like(here)
-            if a < PER_VX - 1:
-                flux = flux + root_up * load(slot, pl.ds(pl.multiple_of((a + 1) * 64 + r, 16), 16))
-            if a > 0:
-                flux = flux + root * load(slot, pl.ds(pl.multiple_of((a - 1) * 64 + r, 16), 16))
+            flux = root_up * load(slot, pl.ds(pl.multiple_of(above + r, 16), 16))
+            flux = flux + root * load(slot, pl.ds(pl.multiple_of(below + r, 16), 16))
             rows = pl.ds(pl.multiple_of(slot * 64 + r, 16), 16)
-            ab_send[0, a, rows, :] = (0.5 * flux - 0.5 * bound_x * here).astype(ab_send.dtype)
-            ab_send[1, a, rows, :] = (-0.5 * flux - 0.5 * bound_x * here).astype(ab_send.dtype)
-            return carry
-
-        lax.fori_loop(0, OWN * 4, part, 0)
+            ab_send[0, a, rows, :] = 0.5 * flux - 0.5 * bound_x * here
+            ab_send[1, a, rows, :] = -0.5 * flux - 0.5 * bound_x * here
+
+        each(OWN * 4, part)
 
     def layer(way, a):
         return pltpu.make_async_remote_copy(
@@ -423,19 +439,33 @@
         def _():
             layer(1, a).start()
 
+    def clear(way):
+        def one(i):
+            wide = ab_recv.shape[2:]
+            ab_recv[way, i // 8, pl.ds(pl.multiple_of(lax.rem(i, 8) * 16, 16), 16), :] = jnp.zeros(
+                (16, wide[1]), F32
+            )
+
+        each(PER_VX * 8, one)
+
+        def edge(i):
+            edge_recv[way, i // OWN, lax.rem(i, OWN)] = jnp.zeros(edge_recv.shape[3:], BF16)
+
+        each(2 * OWN, edge)
+
     @pl.when(sx == space_count - 1)
     def _():
-        ab_recv[0] = jnp.zeros(ab_recv.shape[1:], ab_recv.dtype)
-        edge_recv[0] = jnp.zeros(edge_recv.shape[1:], BF16)
+        clear(0)
 
     @pl.when(sx == 0)
     def _():
-        ab_recv[1] = jnp.zeros(ab_recv.shape[1:], ab_recv.dtype)
-        edge_recv[1] = jnp.zeros(edge_recv.shape[1:], BF16)
-
-    for a in range(PER_VX):
+        clear(1)
+
+    def out_layers(a):
         x_parts(a)
         send_layers(a)
+
+    each(PER_VX, out_layers)
 
     def forward_wait(source, step):
         sender = lax.rem(m + step, SPLIT)
@@ -448,15 +478,16 @@
             device_id_type=MESH,
         ).wait_recv()
 
-    for back in range(SPLIT):
-        source = lax.rem(q + SPLIT - back, SPLIT)
-        for step in range(1, SPLIT):
-            forward_wait(source, step)
+    def arrive(i):
+        source = lax.rem(q + 2 * SPLIT - 1 - i, SPLIT)
+        each(SPLIT - 1, lambda step: forward_wait(source, step + 1))
         picked = dot(pick[...], full[source])
         for slot in range(OWN):
             low[source, :, slot * LANES : (slot + 1) * LANES] = picked[
                 slot * PAD_J : (slot + 1) * PAD_J
             ]
+
+    each(SPLIT, arrive)
 
     def of_species(r):
         return low[r // OWN, :, (r % OWN) * LANES : (r % OWN + 1) * LANES]
@@ -504,22 +535,23 @@
         lax.fori_loop(0, PAD_N // group, some, 0)
         gsend[pair] = gsum[...].astype(BF16)
 
-    for step in (1, 2, 3, 0):
-        pair = lax.rem(q + step, SPLIT)
+    def results(i):
+        pair = lax.rem(q + 1 + i, SPLIT)
         partners(pair)
         collide(pair)
-        for target in range(2):
-            if step > 0:
+
+        def to(target):
+            @pl.when((pair != q) | (m != target))
+            def _():
                 give(pair, target).start()
-            else:
-
-                @pl.when(m != target)
-                def _():
-                    give(pair, target).start()
-
-                @pl.when(m == target)
-                def _():
-                    grecv[q, target * PAD_N : (target + 1) * PAD_N, :] = gsend[pair]
+
+        each(2, to)
+
+    each(SPLIT, results)
+
+    @pl.when(m < 2)
+    def _():
+        grecv[q, pl.ds(pl.multiple_of(m * PAD_N, PAD_N), PAD_N), :] = gsend[q]
 
     @pl.when(m > 0)
     def _():
@@ -555,16 +587,35 @@
     def _():
         edges(1).start()
 
-    for a in range(PER_VX):
-
-        @pl.when(sx < space_count - 1)
+    def spend(slot, rows, term):
+        term = (nu_step * th_ref[slot]) * term
+        for part in range(SPLIT):
+            out_ref[part, slot, rows, :] = (
+                out_ref[part, slot, rows, :] - term[:, part * LANES : (part + 1) * LANES]
+            )
+
+    def add_x(i):
+        a = i // 8
+
+        @pl.when((lax.rem(i, 8) == 0) & (sx < space_count - 1))
         def _():
             layer(0, a).wait_recv()
 
-        @pl.when(sx > 0)
+        @pl.when((lax.rem(i, 8) == 0) & (sx > 0))
         def _():
             layer(1, a).wait_recv()
 
+        slot = lax.rem(i, 8) // 4
+        r = lax.rem(i, 4) * 16
+        rows = pl.ds(pl.multiple_of(slot * 64 + r, 16), 16)
+        spend(
+            slot,
+            pl.ds(pl.multiple_of(a * 64 + r, 16), 16),
+            ab_recv[0, a, rows, :] + ab_recv[1, a, rows, :],
+        )
+
+    each(PER_VX * 8, add_x)
+
     @pl.when(sx < space_count - 1)
     def _():
         edges(0).wait_recv()
@@ -573,28 +624,21 @@
     def _():
         edges(1).wait_recv()
 
-    for a in range(PER_VX):
-        root, root_up = degree_roots(a)
-
-        def add_x(i, carry):
-            slot = i // 4
-            r = pl.multiple_of(lax.rem(i, 4) * 16, 16)
-            rows = pl.ds(pl.multiple_of(slot * 64 + r, 16), 16)
-            here = pl.ds(pl.multiple_of(a * 64 + r, 16), 16)
-            term = ab_recv[0, a, rows, :] + ab_recv[1, a, rows, :]
-            side = {0: 0, PER_VX - 1: 1}.get(a)
-            if side is not None:
-                up = edge_recv[0, side, slot, pl.ds(r, 16), :].astype(F32)
-                down = edge_recv[1, side, slot, pl.ds(r, 16), :].astype(F32)
-                term = term + (0.5 * (root_up if side else root)) * (up - down)
-            term = (nu_step * th_ref[slot]) * term
-            for part in range(SPLIT):
-                out_ref[part, slot, here, :] = (
-                    out_ref[part, slot, here, :] - term[:, part * LANES : (part + 1) * LANES]
-                )
-            return carry
-
-        lax.fori_loop(0, OWN * 4, add_x, 0)
+    def add_edge(i):
+        side = i // 8
+        slot = lax.rem(i, 8) // 4
+        r = pl.multiple_of(lax.rem(i, 4) * 16, 16)
+        degree = jnp.asarray((m + side) * PER_VX, jnp.int32).astype(F32)
+        half = 0.5 * jnp.sqrt(jnp.full((8, 128), degree, F32))[0:1, 0:1]
+        up = edge_recv[0, side, slot, pl.ds(r, 16), :].astype(F32)
+        down = edge_recv[1, side, slot, pl.ds(r, 16), :].astype(F32)
+        spend(
+            slot,
+            pl.ds(pl.multiple_of(side * (ROWS - 64) + r, 16), 16),
+            half * (up - down),
+        )
+
+    each(16, add_edge)
 
     def column_out(part, slot):
         return pltpu.make_async_copy(
@@ -605,51 +649,49 @@
 
     @pl.when(m >= 2)
     def _():
-        for part in range(SPLIT):
-            for slot in range(OWN):
-                column_out(part, slot).start()
+        each(SPLIT * OWN, lambda i: column_out(i // OWN, lax.rem(i, OWN)).start())
+
+    def finish(i):
+        source = lax.rem(q + 2 * SPLIT - 1 - i, SPLIT)
+
+        def take(sender):
+            @pl.when((source != q) | (m != sender))
+            def _():
+                pltpu.make_async_remote_copy(
+                    src_ref=gsend.at[0],
+                    dst_ref=grecv.at[
+                        source, pl.ds(pl.multiple_of(sender * PAD_N, PAD_N), PAD_N)
+                    ],
+                    send_sem=s3.at[0, 0],
+                    recv_sem=r3.at[source, sender],
+                    device_id={"mode": lax.rem(m + 1, SPLIT)},
+                    device_id_type=MESH,
+                ).wait_recv()
+
+        each(SPLIT, take)
+        gained = dot(spread[...], grecv[source])
+        for slot in range(OWN):
+            out_ref[source, slot] = (
+                out_ref[source, slot] + dt_step * gained[:, slot * LANES : (slot + 1) * LANES]
+            )
+            column_out(source, slot).start()
 
     @pl.when(m < 2)
     def _():
-        for back in range(SPLIT):
-            source = lax.rem(q + SPLIT - back, SPLIT)
-            for sender in range(SPLIT):
-
-                def take():
-                    pltpu.make_async_remote_copy(
-                        src_ref=gsend.at[0],
-                        dst_ref=grecv.at[source, pl.ds(sender * PAD_N, PAD_N)],
-                        send_sem=s3.at[0, 0],
-                        recv_sem=r3.at[source, sender],
-                        device_id={"mode": lax.rem(m + 1, SPLIT)},
-                        device_id_type=MESH,
-                    ).wait_recv()
-
-                if back > 0 or sender > 1:
-                    take()
-                else:
-                    pl.when(m != sender)(take)
-            gained = dot(spread[...], grecv[source])
-            for slot in range(OWN):
-                out_ref[source, slot] = (
-                    out_ref[source, slot] + dt_step * gained[:, slot * LANES : (slot + 1) * LANES]
-                )
-                column_out(source, slot).start()
+        each(SPLIT, finish)
 
     @pl.when(m == 0)
     def _():
-        for step in range(SPLIT):
-            for item in head_copies(step):
-                item.wait_send()
+        head_copies(sent)
 
     @pl.when(m == 1)
     def _():
-        for step in range(SPLIT):
-            tail_copies(step).wait_send()
-
-    for back in range(SPLIT):
-        for step in range(1, SPLIT):
-            forward(lax.rem(q + SPLIT - back, SPLIT), step).wait_send()
+        tail_copies(sent)
+
+    each(
+        SPLIT * (SPLIT - 1),
+        lambda i: forward(i // (SPLIT - 1), lax.rem(i, SPLIT - 1) + 1).wait_send(),
+    )
 
     @pl.when(m > 0)
     def _():
@@ -659,38 +701,30 @@
     def _():
         halo(1).wait_send()
 
-    for a in range(PER_VX):
-
-        @pl.when(sx > 0)
+    @pl.when(sx > 0)
+    def _():
+        each(PER_VX, lambda a: layer(0, a).wait_send())
+
+    @pl.when(sx < space_count - 1)
+    def _():
+        each(PER_VX, lambda a: layer(1, a).wait_send())
+
+    @pl.when(sx > 0)
+    def _():
+        edges(0).wait_send()
+
+    @pl.when(sx < space_count - 1)
+    def _():
+        edges(1).wait_send()
+
+    def given(i):
+        @pl.when((i // 2 != q) | (m != lax.rem(i, 2)))
         def _():
-            layer(0, a).wait_send()
-
-        @pl.when(sx < space_count - 1)
-        def _():
-            layer(1, a).wait_send()
-
-    @pl.when(sx > 0)
-    def _():
-        edges(0).wait_send()
-
-    @pl.when(sx < space_count - 1)
-    def _():
-        edges(1).wait_send()
-
-    for step in range(SPLIT):
-        pair = lax.rem(q + step, SPLIT)
-        for target in range(2):
-            if step > 0:
-                give(pair, target).wait_send()
-            else:
-
-                @pl.when(m != target)
-                def _():
-                    give(pair, target).wait_send()
-
-    for part in range(SPLIT):
-        for slot in range(OWN):
-            column_out(part, slot).wait()
+            give(i // 2, lax.rem(i, 2)).wait_send()
+
+    each(SPLIT * 2, given)
+
+    each(SPLIT * OWN, lambda i: column_out(i // OWN, lax.rem(i, OWN)).wait())
 
 
 def write_out(source, result, held, sems):
@@ -743,6 +777,7 @@
             pltpu.VMEM((SPLIT, SPLIT * PAD_N, own * LANES), BF16),
             pltpu.VMEM((own * PAD_J, PACK), BF16),
             pltpu.VMEM((ROWS, PAD_J), BF16),
+            pltpu.VMEM((PACK, own * rows), BF16),
             pltpu.VMEM((2, own, 64, cells), BF16),
             pltpu.VMEM((2, own, 64, cells), BF16),
             pltpu.VMEM((2, 2, own, 64, cells), BF16),

time: 29.5 us -> 32.2 us (1.092)
  Pallas kernels: 29.3 us -> 32.1 us
    pallas_call x1, Pallas kernels: 27.3 us -> 30.1 us  [per_device(): pl.pallas_call(functools.partial(kernel, space_count), out_shape=jax.Shap...]
where the time goes in v5:
time: 32.2 us; the launch traced here: 32.1 us
  Pallas kernels  32.1 us (100%)
    pallas_call x1, Pallas kernels, per_device(): pl.pallas_call(functools.partial(kernel, space_count), out_shape=jax.Shap...  30.1 us
    pallas_call x1, Pallas kernels, per_device(): pl.pallas_call(write_out, out_shape=jax.ShapeDtypeStruct(distribution.sha...  1.98 us

profile of v5, /device:TPU:0, one launch (start us, length us, event | category | flops | bytes accessed | tf_op | source)
XLA Modules:
  0.0 32.1 jit_solution(14006933319654151055)
XLA Ops:
  0.0 30.1 %shard_map.73.source = f32[2,256,1,512]{3,2,1,0:T(1,128)} custom-call(f32[2,256,1,512]{3,2,1,0:T(1,128)} %f_in.1, bf16[2,30,120,120]{3,2,1,0:T(8,128)(2,1)} %k_in.1, s32[256,8]{1,0:T(8,128)} %constant.2.clone.tab_in, s32[1,120]{1,0:T(1,128)} %bitcast.1, s32[8,8]{1,0:T(8,128)} %kind_in.1, f32[2]{0:T(128)} %th_in.1, f32[2]{0:T(128)} %rx_in.1), custom_call_target="tpu_custom_call" | custom-call | tf_op jit(solution)/shard_map/pallas_call | solution.py:755
  30.1 2.0 %shard_map.74 = f32[2,256,1,512]{3,2,1,0:T(1,128)} custom-call(f32[2,256,1,512]{3,2,1,0:T(1,128)} %shard_map.73.source), custom_call_target="tpu_custom_call" | custom-call | tf_op jit(solution)/shard_map/pallas_call | solution.py:813

commit v6 on v3

--- a/solution.py
+++ b/solution.py
@@ -186,12 +186,12 @@
     def _():
         pl.semaphore_wait(barrier, peers + min(1, space_count - 1))
 
-    def scatter(part, piece, first, count, source):
+    def scatter(part, piece, first, count):
         return pltpu.make_async_remote_copy(
             src_ref=low_send.at[part, pl.ds(first, count)],
             dst_ref=full.at[q, pl.ds(first, count)],
-            send_sem=s1.at[part, piece],
-            recv_sem=r1.at[q, source],
+            send_sem=s1,
+            recv_sem=r1.at[q],
             device_id={"species": part, "mode": piece},
             device_id_type=MESH,
         )
@@ -205,11 +205,11 @@
             if step == 0 and piece == 0:
                 continue
             count = PIECE if piece < 3 else head_last
-            found.append(scatter(part, piece, piece * PIECE, count, 0))
+            found.append(scatter(part, piece, piece * PIECE, count))
         return found
 
     def tail_copies(step):
-        return scatter(lax.rem(q + step, SPLIT), 3, HEAD, PACK - HEAD, 1)
+        return scatter(lax.rem(q + step, SPLIT), 3, HEAD, PACK - HEAD)
 
     @pl.when(m == 0)
     def _():
@@ -283,47 +283,39 @@
     mode_of = lax.broadcasted_iota(jnp.int32, (ROWS, PAD_J), 0) + m * ROWS
     spread[...] = jnp.where(mode_of == by_block[0:1, :], 1.0, 0.0).astype(BF16)
 
-    def piece_wait(source, count, sender):
+    def piece_wait(source):
         pltpu.make_async_remote_copy(
-            src_ref=low_send.at[0, pl.ds(0, count)],
-            dst_ref=full.at[source, pl.ds(0, count)],
-            send_sem=s1.at[0, 0],
-            recv_sem=r1.at[source, sender],
+            src_ref=low_send.at[0, pl.ds(0, PIECE)],
+            dst_ref=full.at[source, pl.ds(0, PIECE)],
+            send_sem=s1,
+            recv_sem=r1.at[source],
             device_id={"mode": lax.rem(m + 1, SPLIT)},
             device_id_type=MESH,
         ).wait_recv()
 
-    def forward(source, step):
+    def forward(half, step):
         rows = pl.ds(pl.multiple_of(m * PIECE, PIECE), PIECE)
         return pltpu.make_async_remote_copy(
-            src_ref=full.at[source, rows],
-            dst_ref=full.at[source, rows],
-            send_sem=s2.at[source, step],
-            recv_sem=r2.at[source, m],
+            src_ref=full.at[pl.ds(half * 2, 2), rows],
+            dst_ref=full.at[pl.ds(half * 2, 2), rows],
+            send_sem=s2,
+            recv_sem=r2.at[half],
             device_id={"mode": lax.rem(m + step, SPLIT)},
             device_id_type=MESH,
         )
 
-    for back in range(SPLIT):
-        source = lax.rem(q + SPLIT - back, SPLIT)
-
-        if back > 0:
-
-            @pl.when(m == 0)
+    near = q // 2
+    halves = (near, 1 - near)
+    for half in halves:
+        for spot in range(2):
+            source = half * 2 + spot
+
+            @pl.when((m > 0) | (source != q))
             def _():
-                piece_wait(source, PIECE, 0)
-
-        @pl.when((m == 1) | (m == 2))
-        def _():
-            piece_wait(source, PIECE, 0)
-
-        @pl.when(m == 3)
-        def _():
-            piece_wait(source, head_last, 0)
-            piece_wait(source, PACK - HEAD, 1)
-
-        for step in range(1, SPLIT):
-            forward(source, step).start()
+                piece_wait(source)
+
+        for step in (2, 1, 3):
+            forward(half, step).start()
 
     @pl.when(m < 2)
     def _():
@@ -404,24 +396,15 @@
 
         lax.fori_loop(0, OWN * 4, part, 0)
 
-    def layer(way, a):
+    def layer(way):
         return pltpu.make_async_remote_copy(
-            src_ref=ab_send.at[way, a],
-            dst_ref=ab_recv.at[way, a],
-            send_sem=xs.at[way, a],
-            recv_sem=xr.at[way, a],
+            src_ref=ab_send.at[way],
+            dst_ref=ab_recv.at[way],
+            send_sem=xs.at[way],
+            recv_sem=xr.at[way],
             device_id={"space": sx - 1 if way == 0 else sx + 1},
             device_id_type=MESH,
         )
-
-    def send_layers(a):
-        @pl.when(sx > 0)
-        def _():
-            layer(0, a).start()
-
-        @pl.when(sx < space_count - 1)
-        def _():
-            layer(1, a).start()
 
     @pl.when(sx == space_count - 1)
     def _():
@@ -435,28 +418,35 @@
 
     for a in range(PER_VX):
         x_parts(a)
-        send_layers(a)
-
-    def forward_wait(source, step):
-        sender = lax.rem(m + step, SPLIT)
+
+    @pl.when(sx > 0)
+    def _():
+        layer(0).start()
+
+    @pl.when(sx < space_count - 1)
+    def _():
+        layer(1).start()
+
+    def forward_wait(half):
+        others = full.at[pl.ds(half * 2, 2), pl.ds(0, 3 * PIECE)]
         pltpu.make_async_remote_copy(
-            src_ref=full.at[source, pl.ds(0, PIECE)],
-            dst_ref=full.at[source, pl.ds(0, PIECE)],
-            send_sem=s2.at[source, step],
-            recv_sem=r2.at[source, sender],
-            device_id={"mode": sender},
+            src_ref=others,
+            dst_ref=others,
+            send_sem=s2,
+            recv_sem=r2.at[half],
+            device_id={"mode": lax.rem(m + 1, SPLIT)},
             device_id_type=MESH,
         ).wait_recv()
 
-    for back in range(SPLIT):
-        source = lax.rem(q + SPLIT - back, SPLIT)
-        for step in range(1, SPLIT):
-            forward_wait(source, step)
-        picked = dot(pick[...], full[source])
-        for slot in range(OWN):
-            low[source, :, slot * LANES : (slot + 1) * LANES] = picked[
-                slot * PAD_J : (slot + 1) * PAD_J
-            ]
+    for half in halves:
+        forward_wait(half)
+        for spot in range(2):
+            source = half * 2 + spot
+            picked = dot(pick[...], full[source])
+            for slot in range(OWN):
+                low[source, :, slot * LANES : (slot + 1) * LANES] = picked[
+                    slot * PAD_J : (slot + 1) * PAD_J
+                ]
 
     def of_species(r):
         return low[r // OWN, :, (r % OWN) * LANES : (r % OWN + 1) * LANES]
@@ -483,8 +473,8 @@
         return pltpu.make_async_remote_copy(
             src_ref=gsend.at[pair],
             dst_ref=grecv.at[q, pl.ds(pl.multiple_of(m * PAD_N, PAD_N), PAD_N)],
-            send_sem=s3.at[pair, target],
-            recv_sem=r3.at[q, m],
+            send_sem=s3,
+            recv_sem=r3.at[q],
             device_id={"species": pair, "mode": target},
             device_id_type=MESH,
         )
@@ -555,22 +545,14 @@
     def _():
         edges(1).start()
 
-    for a in range(PER_VX):
-
-        @pl.when(sx < space_count - 1)
-        def _():
-            layer(0, a).wait_recv()
-
-        @pl.when(sx > 0)
-        def _():
-            layer(1, a).wait_recv()
-
     @pl.when(sx < space_count - 1)
     def _():
+        layer(0).wait_recv()
         edges(0).wait_recv()
 
     @pl.when(sx > 0)
     def _():
+        layer(1).wait_recv()
         edges(1).wait_recv()
 
     for a in range(PER_VX):
@@ -611,24 +593,17 @@
 
     @pl.when(m < 2)
     def _():
-        for back in range(SPLIT):
+        for back in (1, 2, 3, 0):
             source = lax.rem(q + SPLIT - back, SPLIT)
-            for sender in range(SPLIT):
-
-                def take():
-                    pltpu.make_async_remote_copy(
-                        src_ref=gsend.at[0],
-                        dst_ref=grecv.at[source, pl.ds(sender * PAD_N, PAD_N)],
-                        send_sem=s3.at[0, 0],
-                        recv_sem=r3.at[source, sender],
-                        device_id={"mode": lax.rem(m + 1, SPLIT)},
-                        device_id_type=MESH,
-                    ).wait_recv()
-
-                if back > 0 or sender > 1:
-                    take()
-                else:
-                    pl.when(m != sender)(take)
+            came = grecv.at[source, pl.ds(0, (SPLIT if back else SPLIT - 1) * PAD_N)]
+            pltpu.make_async_remote_copy(
+                src_ref=came,
+                dst_ref=came,
+                send_sem=s3,
+                recv_sem=r3.at[source],
+                device_id={"mode": lax.rem(m + 1, SPLIT)},
+                device_id_type=MESH,
+            ).wait_recv()
             gained = dot(spread[...], grecv[source])
             for slot in range(OWN):
                 out_ref[source, slot] = (
@@ -636,20 +611,25 @@
                 )
                 column_out(source, slot).start()
 
+    def all_sent(rows, sem):
+        pltpu.make_async_remote_copy(
+            src_ref=rows,
+            dst_ref=rows,
+            send_sem=sem,
+            recv_sem=r1.at[0],
+            device_id={"mode": lax.rem(m + 1, SPLIT)},
+            device_id_type=MESH,
+        ).wait_send()
+
     @pl.when(m == 0)
     def _():
-        for step in range(SPLIT):
-            for item in head_copies(step):
-                item.wait_send()
+        all_sent(low_send.at[:, pl.ds(0, HEAD - PIECE // SPLIT)], s1)
 
     @pl.when(m == 1)
     def _():
-        for step in range(SPLIT):
-            tail_copies(step).wait_send()
-
-    for back in range(SPLIT):
-        for step in range(1, SPLIT):
-            forward(lax.rem(q + SPLIT - back, SPLIT), step).wait_send()
+        all_sent(low_send.at[:, pl.ds(0, PACK - HEAD)], s1)
+
+    all_sent(full.at[:, pl.ds(0, 3 * PIECE)], s2)
 
     @pl.when(m > 0)
     def _():
@@ -659,34 +639,29 @@
     def _():
         halo(1).wait_send()
 
-    for a in range(PER_VX):
-
-        @pl.when(sx > 0)
-        def _():
-            layer(0, a).wait_send()
-
-        @pl.when(sx < space_count - 1)
-        def _():
-            layer(1, a).wait_send()
-
     @pl.when(sx > 0)
     def _():
+        layer(0).wait_send()
+
+    @pl.when(sx < space_count - 1)
+    def _():
+        layer(1).wait_send()
+
+    @pl.when(sx > 0)
+    def _():
         edges(0).wait_send()
 
     @pl.when(sx < space_count - 1)
     def _():
         edges(1).wait_send()
 
-    for step in range(SPLIT):
-        pair = lax.rem(q + step, SPLIT)
-        for target in range(2):
-            if step > 0:
-                give(pair, target).wait_send()
-            else:
-
-                @pl.when(m != target)
-                def _():
-                    give(pair, target).wait_send()
+    @pl.when(m < 2)
+    def _():
+        all_sent(grecv.at[pl.ds(0, 2), pl.ds(0, 7 * PAD_N // 2)], s3)
+
+    @pl.when(m >= 2)
+    def _():
+        all_sent(grecv.at[pl.ds(0, 2)], s3)
 
     for part in range(SPLIT):
         for slot in range(OWN):
@@ -750,16 +725,16 @@
             pltpu.VMEM((2, PER_VX, own * 64, cells), ab_type),
             dma((SPLIT, OWN)),
             dma((6,)),
-            dma((SPLIT, SPLIT)),
-            dma((SPLIT, 2)),
-            dma((SPLIT, SPLIT)),
-            dma((SPLIT, SPLIT)),
-            dma((SPLIT, 2)),
-            dma((SPLIT, SPLIT)),
+            dma,
+            dma((SPLIT,)),
+            dma,
+            dma((2,)),
+            dma,
+            dma((SPLIT,)),
             dma((2,)),
             dma((2,)),
-            dma((2, PER_VX)),
-            dma((2, PER_VX)),
+            dma((2,)),
+            dma((2,)),
             dma((2,)),
             dma((2,)),
         ],

time: 29.5 us -> 29.5 us (level)
  no operation moved by 1% of the time
where the time goes in v6:
time: 29.5 us; the launch traced here: 29.3 us
  Pallas kernels  29.3 us (99%)
    pallas_call x1, Pallas kernels, per_device(): pl.pallas_call(functools.partial(kernel, space_count), out_shape=jax.Shap...  27.3 us
    pallas_call x1, Pallas kernels, per_device(): pl.pallas_call(write_out, out_shape=jax.ShapeDtypeStruct(distribution.sha...  1.98 us

profile of v6, /device:TPU:0, one launch (start us, length us, event | category | flops | bytes accessed | tf_op | source)
XLA Modules:
  0.0 29.3 jit_solution(203608490505350982)
XLA Ops:
  0.0 27.3 %shard_map.73.source = f32[2,256,1,512]{3,2,1,0:T(1,128)} custom-call(f32[2,256,1,512]{3,2,1,0:T(1,128)} %f_in.1, bf16[2,30,120,120]{3,2,1,0:T(8,128)(2,1)} %k_in.1, s32[256,8]{1,0:T(8,128)} %constant.2.clone.tab_in, s32[1,120]{1,0:T(1,128)} %bitcast.1, s32[8,8]{1,0:T(8,128)} %kind_in.1, f32[2]{0:T(128)} %th_in.1, f32[2]{0:T(128)} %rx_in.1), custom_call_target="tpu_custom_call" | custom-call | tf_op jit(solution)/shard_map/pallas_call | solution.py:696
  27.4 2.0 %shard_map.74 = f32[2,256,1,512]{3,2,1,0:T(1,128)} custom-call(f32[2,256,1,512]{3,2,1,0:T(1,128)} %shard_map.73.source), custom_call_target="tpu_custom_call" | custom-call | tf_op jit(solution)/shard_map/pallas_call | solution.py:753

commit v7 on v6

--- a/solution.py
+++ b/solution.py
@@ -245,6 +245,48 @@
     def _():
         halo(1).start()
 
+    def piece_wait(source):
+        pltpu.make_async_remote_copy(
+            src_ref=low_send.at[0, pl.ds(0, PIECE)],
+            dst_ref=full.at[source, pl.ds(0, PIECE)],
+            send_sem=s1,
+            recv_sem=r1.at[source],
+            device_id={"mode": lax.rem(m + 1, SPLIT)},
+            device_id_type=MESH,
+        ).wait_recv()
+
+    def forward(half, step):
+        rows = pl.ds(pl.multiple_of(m * PIECE, PIECE), PIECE)
+        return pltpu.make_async_remote_copy(
+            src_ref=full.at[pl.ds(half * 2, 2), rows],
+            dst_ref=full.at[pl.ds(half * 2, 2), rows],
+            send_sem=s2,
+            recv_sem=r2.at[half],
+            device_id={"mode": lax.rem(m + step, SPLIT)},
+            device_id_type=MESH,
+        )
+
+    near = q // 2
+    halves = (near, 1 - near)
+    for half in halves:
+        for spot in range(2):
+            source = half * 2 + spot
+
+            @pl.when((m > 0) | (source != q))
+            def _():
+                piece_wait(source)
+
+        for step in (2, 1, 3):
+            forward(half, step).start()
+
+    @pl.when(m < 2)
+    def _():
+        halo(1).start()
+
+    @pl.when(m == 2)
+    def _():
+        halo(0).start()
+
     for item in small[1:] + [copy_k]:
         item.wait()
 
@@ -280,50 +322,145 @@
     for slot in range(OWN):
         same = tab_ref[:, 1 + slot : 2 + slot] == ordered[0:1, :]
         pick[slot * PAD_J : (slot + 1) * PAD_J, :] = jnp.where(same, 1.0, 0.0).T.astype(BF16)
-    mode_of = lax.broadcasted_iota(jnp.int32, (ROWS, PAD_J), 0) + m * ROWS
-    spread[...] = jnp.where(mode_of == by_block[0:1, :], 1.0, 0.0).astype(BF16)
-
-    def piece_wait(source):
+    def degree_roots(a):
+        degree = (m * PER_VX + a).astype(F32)
+        below = jnp.sqrt(jnp.full((8, 128), degree, F32))[0:1, 0:1]
+        above = jnp.sqrt(jnp.full((8, 128), degree + 1.0, F32))[0:1, 0:1]
+        return below, above
+
+    def x_parts(a):
+        root, root_up = degree_roots(a)
+
+        def part(i, carry):
+            slot = i // 4
+            r = lax.rem(i, 4) * 16
+            here = load(slot, pl.ds(pl.multiple_of(a * 64 + r, 16), 16))
+            flux = jnp.zeros_like(here)
+            if a < PER_VX - 1:
+                flux = flux + root_up * load(slot, pl.ds(pl.multiple_of((a + 1) * 64 + r, 16), 16))
+            if a > 0:
+                flux = flux + root * load(slot, pl.ds(pl.multiple_of((a - 1) * 64 + r, 16), 16))
+            rows = pl.ds(pl.multiple_of(slot * 64 + r, 16), 16)
+            ab_send[0, a, rows, :] = (0.5 * flux - 0.5 * bound_x * here).astype(ab_send.dtype)
+            ab_send[1, a, rows, :] = (-0.5 * flux - 0.5 * bound_x * here).astype(ab_send.dtype)
+            return carry
+
+        lax.fori_loop(0, OWN * 4, part, 0)
+
+    def layer(way):
+        return pltpu.make_async_remote_copy(
+            src_ref=ab_send.at[way],
+            dst_ref=ab_recv.at[way],
+            send_sem=xs.at[way],
+            recv_sem=xr.at[way],
+            device_id={"space": sx - 1 if way == 0 else sx + 1},
+            device_id_type=MESH,
+        )
+
+    @pl.when(sx == space_count - 1)
+    def _():
+        ab_recv[0] = jnp.zeros(ab_recv.shape[1:], ab_recv.dtype)
+        edge_recv[0] = jnp.zeros(edge_recv.shape[1:], BF16)
+
+    @pl.when(sx == 0)
+    def _():
+        ab_recv[1] = jnp.zeros(ab_recv.shape[1:], ab_recv.dtype)
+        edge_recv[1] = jnp.zeros(edge_recv.shape[1:], BF16)
+
+    for a in range(PER_VX):
+        x_parts(a)
+
+    @pl.when(sx > 0)
+    def _():
+        layer(0).start()
+
+    @pl.when(sx < space_count - 1)
+    def _():
+        layer(1).start()
+
+    def forward_wait(half):
+        others = full.at[pl.ds(half * 2, 2), pl.ds(0, 3 * PIECE)]
         pltpu.make_async_remote_copy(
-            src_ref=low_send.at[0, pl.ds(0, PIECE)],
-            dst_ref=full.at[source, pl.ds(0, PIECE)],
-            send_sem=s1,
-            recv_sem=r1.at[source],
-            device_id={"mode": lax.rem(m + 1, SPLIT)},
-            device_id_type=MESH,
-        ).wait_recv()
-
-    def forward(half, step):
-        rows = pl.ds(pl.multiple_of(m * PIECE, PIECE), PIECE)
-        return pltpu.make_async_remote_copy(
-            src_ref=full.at[pl.ds(half * 2, 2), rows],
-            dst_ref=full.at[pl.ds(half * 2, 2), rows],
+            src_ref=others,
+            dst_ref=others,
             send_sem=s2,
             recv_sem=r2.at[half],
-            device_id={"mode": lax.rem(m + step, SPLIT)},
-            device_id_type=MESH,
-        )
-
-    near = q // 2
-    halves = (near, 1 - near)
+            device_id={"mode": lax.rem(m + 1, SPLIT)},
+            device_id_type=MESH,
+        ).wait_recv()
+
     for half in halves:
+        forward_wait(half)
         for spot in range(2):
             source = half * 2 + spot
-
-            @pl.when((m > 0) | (source != q))
-            def _():
-                piece_wait(source)
-
-        for step in (2, 1, 3):
-            forward(half, step).start()
-
-    @pl.when(m < 2)
-    def _():
-        halo(1).start()
-
-    @pl.when(m == 2)
-    def _():
-        halo(0).start()
+            picked = dot(pick[...], full[source])
+            for slot in range(OWN):
+                low[source, :, slot * LANES : (slot + 1) * LANES] = picked[
+                    slot * PAD_J : (slot + 1) * PAD_J
+                ]
+
+    def of_species(r):
+        return low[r // OWN, :, (r % OWN) * LANES : (r % OWN + 1) * LANES]
+
+    everyone = of_species(0)
+    for r in range(1, SPLIT * OWN):
+        everyone = everyone + of_species(r)
+    total[...] = everyone
+
+    def partners(pair):
+        def one(slot):
+            first = jnp.zeros((PAD_J, LANES), F32)
+            for r in range(SPLIT * OWN):
+                weight = jnp.where(kind_ref[pair * OWN + slot, r] == 0, 1.0, 0.0)
+                first = first + weight * of_species(r)
+            cut = slice(slot * LANES, (slot + 1) * LANES)
+            pmat[pair, 0:PAD_J, cut] = first.astype(BF16)
+            pmat[pair, PAD_J:, cut] = (total[...] - first).astype(BF16)
+
+        for slot in range(OWN):
+            one(slot)
+
+    def give(pair, target):
+        return pltpu.make_async_remote_copy(
+            src_ref=gsend.at[pair],
+            dst_ref=grecv.at[q, pl.ds(pl.multiple_of(m * PAD_N, PAD_N), PAD_N)],
+            send_sem=s3,
+            recv_sem=r3.at[q],
+            device_id={"species": pair, "mode": target},
+            device_id_type=MESH,
+        )
+
+    group = 8
+
+    def collide(pair):
+        def some(i, carry):
+            left = k2[pl.ds(pl.multiple_of(i * group, group), group)]
+            product = dot(left.reshape(group * PAD_J, NKIND * PAD_J), pmat[pair])
+            own = low[pair]
+            gsum[pl.ds(pl.multiple_of(i * group, group), group), :] = jnp.sum(
+                product.reshape(group, PAD_J, OWN * LANES) * own[None], axis=1
+            )
+            return carry
+
+        lax.fori_loop(0, PAD_N // group, some, 0)
+        gsend[pair] = gsum[...].astype(BF16)
+
+    for step in (1, 2, 3, 0):
+        pair = lax.rem(q + step, SPLIT)
+        partners(pair)
+        collide(pair)
+        for target in range(2):
+            if step > 0:
+                give(pair, target).start()
+            else:
+
+                @pl.when(m != target)
+                def _():
+                    give(pair, target).start()
+
+                @pl.when(m == target)
+                def _():
+                    grecv[q, target * PAD_N : (target + 1) * PAD_N, :] = gsend[pair]
 
     degree_c = lax.broadcasted_iota(jnp.int32, (NVZ, 1), 0)
     sqrt_c = jnp.sqrt(degree_c.astype(F32))
@@ -371,145 +508,8 @@
 
     lax.fori_loop(0, OWN * PER_VX, own_terms, 0)
 
-    def degree_roots(a):
-        degree = (m * PER_VX + a).astype(F32)
-        below = jnp.sqrt(jnp.full((8, 128), degree, F32))[0:1, 0:1]
-        above = jnp.sqrt(jnp.full((8, 128), degree + 1.0, F32))[0:1, 0:1]
-        return below, above
-
-    def x_parts(a):
-        root, root_up = degree_roots(a)
-
-        def part(i, carry):
-            slot = i // 4
-            r = lax.rem(i, 4) * 16
-            here = load(slot, pl.ds(pl.multiple_of(a * 64 + r, 16), 16))
-            flux = jnp.zeros_like(here)
-            if a < PER_VX - 1:
-                flux = flux + root_up * load(slot, pl.ds(pl.multiple_of((a + 1) * 64 + r, 16), 16))
-            if a > 0:
-                flux = flux + root * load(slot, pl.ds(pl.multiple_of((a - 1) * 64 + r, 16), 16))
-            rows = pl.ds(pl.multiple_of(slot * 64 + r, 16), 16)
-            ab_send[0, a, rows, :] = (0.5 * flux - 0.5 * bound_x * here).astype(ab_send.dtype)
-            ab_send[1, a, rows, :] = (-0.5 * flux - 0.5 * bound_x * here).astype(ab_send.dtype)
-            return carry
-
-        lax.fori_loop(0, OWN * 4, part, 0)
-
-    def layer(way):
-        return pltpu.make_async_remote_copy(
-            src_ref=ab_send.at[way],
-            dst_ref=ab_recv.at[way],
-            send_sem=xs.at[way],
-            recv_sem=xr.at[way],
-            device_id={"space": sx - 1 if way == 0 else sx + 1},
-            device_id_type=MESH,
-        )
-
-    @pl.when(sx == space_count - 1)
-    def _():
-        ab_recv[0] = jnp.zeros(ab_recv.shape[1:], ab_recv.dtype)
-        edge_recv[0] = jnp.zeros(edge_recv.shape[1:], BF16)
-
-    @pl.when(sx == 0)
-    def _():
-        ab_recv[1] = jnp.zeros(ab_recv.shape[1:], ab_recv.dtype)
-        edge_recv[1] = jnp.zeros(edge_recv.shape[1:], BF16)
-
-    for a in range(PER_VX):
-        x_parts(a)
-
-    @pl.when(sx > 0)
-    def _():
-        layer(0).start()
-
-    @pl.when(sx < space_count - 1)
-    def _():
-        layer(1).start()
-
-    def forward_wait(half):
-        others = full.at[pl.ds(half * 2, 2), pl.ds(0, 3 * PIECE)]
-        pltpu.make_async_remote_copy(
-            src_ref=others,
-            dst_ref=others,
-            send_sem=s2,
-            recv_sem=r2.at[half],
-            device_id={"mode": lax.rem(m + 1, SPLIT)},
-            device_id_type=MESH,
-        ).wait_recv()
-
-    for half in halves:
-        forward_wait(half)
-        for spot in range(2):
-            source = half * 2 + spot
-            picked = dot(pick[...], full[source])
-            for slot in range(OWN):
-                low[source, :, slot * LANES : (slot + 1) * LANES] = picked[
-                    slot * PAD_J : (slot + 1) * PAD_J
-                ]
-
-    def of_species(r):
-        return low[r // OWN, :, (r % OWN) * LANES : (r % OWN + 1) * LANES]
-
-    everyone = of_species(0)
-    for r in range(1, SPLIT * OWN):
-        everyone = everyone + of_species(r)
-    total[...] = everyone
-
-    def partners(pair):
-        def one(slot):
-            first = jnp.zeros((PAD_J, LANES), F32)
-            for r in range(SPLIT * OWN):
-                weight = jnp.where(kind_ref[pair * OWN + slot, r] == 0, 1.0, 0.0)
-                first = first + weight * of_species(r)
-            cut = slice(slot * LANES, (slot + 1) * LANES)
-            pmat[pair, 0:PAD_J, cut] = first.astype(BF16)
-            pmat[pair, PAD_J:, cut] = (total[...] - first).astype(BF16)
-
-        for slot in range(OWN):
-            one(slot)
-
-    def give(pair, target):
-        return pltpu.make_async_remote_copy(
-            src_ref=gsend.at[pair],
-            dst_ref=grecv.at[q, pl.ds(pl.multiple_of(m * PAD_N, PAD_N), PAD_N)],
-            send_sem=s3,
-            recv_sem=r3.at[q],
-            device_id={"species": pair, "mode": target},
-            device_id_type=MESH,
-        )
-
-    group = 8
-
-    def collide(pair):
-        def some(i, carry):
-            left = k2[pl.ds(pl.multiple_of(i * group, group), group)]
-            product = dot(left.reshape(group * PAD_J, NKIND * PAD_J), pmat[pair])
-            own = low[pair]
-            gsum[pl.ds(pl.multiple_of(i * group, group), group), :] = jnp.sum(
-                product.reshape(group, PAD_J, OWN * LANES) * own[None], axis=1
-            )
-            return carry
-
-        lax.fori_loop(0, PAD_N // group, some, 0)
-        gsend[pair] = gsum[...].astype(BF16)
-
-    for step in (1, 2, 3, 0):
-        pair = lax.rem(q + step, SPLIT)
-        partners(pair)
-        collide(pair)
-        for target in range(2):
-            if step > 0:
-                give(pair, target).start()
-            else:
-
-                @pl.when(m != target)
-                def _():
-                    give(pair, target).start()
-
-                @pl.when(m == target)
-                def _():
-                    grecv[q, target * PAD_N : (target + 1) * PAD_N, :] = gsend[pair]
+    mode_of = lax.broadcasted_iota(jnp.int32, (ROWS, PAD_J), 0) + m * ROWS
+    spread[...] = jnp.where(mode_of == by_block[0:1, :], 1.0, 0.0).astype(BF16)
 
     @pl.when(m > 0)
     def _():

time: 29.5 us -> 29.5 us (level)
  no operation moved by 1% of the time
where the time goes in v7:
time: 29.5 us; the launch traced here: 29.3 us
  Pallas kernels  29.3 us (99%)
    pallas_call x1, Pallas kernels, per_device(): pl.pallas_call(functools.partial(kernel, space_count), out_shape=jax.Shap...  27.3 us
    pallas_call x1, Pallas kernels, per_device(): pl.pallas_call(write_out, out_shape=jax.ShapeDtypeStruct(distribution.sha...  1.98 us

profile of v7, /device:TPU:0, one launch (start us, length us, event | category | flops | bytes accessed | tf_op | source)
XLA Modules:
  0.0 29.3 jit_solution(5657793727213247693)
XLA Ops:
  0.0 27.3 %shard_map.73.source = f32[2,256,1,512]{3,2,1,0:T(1,128)} custom-call(f32[2,256,1,512]{3,2,1,0:T(1,128)} %f_in.1, bf16[2,30,120,120]{3,2,1,0:T(8,128)(2,1)} %k_in.1, s32[256,8]{1,0:T(8,128)} %constant.2.clone.tab_in, s32[1,120]{1,0:T(1,128)} %bitcast.1, s32[8,8]{1,0:T(8,128)} %kind_in.1, f32[2]{0:T(128)} %th_in.1, f32[2]{0:T(128)} %rx_in.1), custom_call_target="tpu_custom_call" | custom-call | tf_op jit(solution)/shard_map/pallas_call | solution.py:696
  27.4 2.0 %shard_map.74 = f32[2,256,1,512]{3,2,1,0:T(1,128)} custom-call(f32[2,256,1,512]{3,2,1,0:T(1,128)} %shard_map.73.source), custom_call_target="tpu_custom_call" | custom-call | tf_op jit(solution)/shard_map/pallas_call | solution.py:753

commit v8 on v6

--- a/solution.py
+++ b/solution.py
@@ -317,14 +317,6 @@
         for step in (2, 1, 3):
             forward(half, step).start()
 
-    @pl.when(m < 2)
-    def _():
-        halo(1).start()
-
-    @pl.when(m == 2)
-    def _():
-        halo(0).start()
-
     degree_c = lax.broadcasted_iota(jnp.int32, (NVZ, 1), 0)
     sqrt_c = jnp.sqrt(degree_c.astype(F32))
     sqrt_c_up = jnp.where(degree_c == NVZ - 1, 0.0, jnp.sqrt(degree_c.astype(F32) + 1.0))
@@ -447,6 +439,14 @@
                 low[source, :, slot * LANES : (slot + 1) * LANES] = picked[
                     slot * PAD_J : (slot + 1) * PAD_J
                 ]
+
+    @pl.when(m < 2)
+    def _():
+        halo(1).start()
+
+    @pl.when(m == 2)
+    def _():
+        halo(0).start()
 
     def of_species(r):
         return low[r // OWN, :, (r % OWN) * LANES : (r % OWN + 1) * LANES]

time: 29.5 us -> 28 us (0.949)
  Pallas kernels: 29.3 us -> 27.8 us
    pallas_call x1, Pallas kernels: 27.3 us -> 25.8 us  [per_device(): pl.pallas_call(functools.partial(kernel, space_count), out_shape=jax.Shap...]
where the time goes in v8:
time: 28 us; the launch traced here: 27.8 us
  Pallas kernels  27.8 us (99%)
    pallas_call x1, Pallas kernels, per_device(): pl.pallas_call(functools.partial(kernel, space_count), out_shape=jax.Shap...  25.8 us
    pallas_call x1, Pallas kernels, per_device(): pl.pallas_call(write_out, out_shape=jax.ShapeDtypeStruct(distribution.sha...  1.98 us

profile of v8, /device:TPU:0, one launch (start us, length us, event | category | flops | bytes accessed | tf_op | source)
XLA Modules:
  0.0 27.8 jit_solution(5056857454462324102)
XLA Ops:
  0.0 25.8 %shard_map.73.source = f32[2,256,1,512]{3,2,1,0:T(1,128)} custom-call(f32[2,256,1,512]{3,2,1,0:T(1,128)} %f_in.1, bf16[2,30,120,120]{3,2,1,0:T(8,128)(2,1)} %k_in.1, s32[256,8]{1,0:T(8,128)} %constant.2.clone.tab_in, s32[1,120]{1,0:T(1,128)} %bitcast.1, s32[8,8]{1,0:T(8,128)} %kind_in.1, f32[2]{0:T(128)} %th_in.1, f32[2]{0:T(128)} %rx_in.1), custom_call_target="tpu_custom_call" | custom-call | tf_op jit(solution)/shard_map/pallas_call | solution.py:696
  25.8 2.0 %shard_map.74 = f32[2,256,1,512]{3,2,1,0:T(1,128)} custom-call(f32[2,256,1,512]{3,2,1,0:T(1,128)} %shard_map.73.source), custom_call_target="tpu_custom_call" | custom-call | tf_op jit(solution)/shard_map/pallas_call | solution.py:753

commit v9 on v8

--- a/solution.py
+++ b/solution.py
@@ -411,14 +411,6 @@
     for a in range(PER_VX):
         x_parts(a)
 
-    @pl.when(sx > 0)
-    def _():
-        layer(0).start()
-
-    @pl.when(sx < space_count - 1)
-    def _():
-        layer(1).start()
-
     def forward_wait(half):
         others = full.at[pl.ds(half * 2, 2), pl.ds(0, 3 * PIECE)]
         pltpu.make_async_remote_copy(
@@ -447,6 +439,14 @@
     @pl.when(m == 2)
     def _():
         halo(0).start()
+
+    @pl.when(sx > 0)
+    def _():
+        layer(0).start()
+
+    @pl.when(sx < space_count - 1)
+    def _():
+        layer(1).start()
 
     def of_species(r):
         return low[r // OWN, :, (r % OWN) * LANES : (r % OWN + 1) * LANES]

time: 28 us -> 28 us (level)
  no operation moved by 1% of the time
where the time goes in v9:
time: 28 us; the launch traced here: 27.8 us
  Pallas kernels  27.8 us (99%)
    pallas_call x1, Pallas kernels, per_device(): pl.pallas_call(functools.partial(kernel, space_count), out_shape=jax.Shap...  25.8 us
    pallas_call x1, Pallas kernels, per_device(): pl.pallas_call(write_out, out_shape=jax.ShapeDtypeStruct(distribution.sha...  1.98 us

profile of v9, /device:TPU:0, one launch (start us, length us, event | category | flops | bytes accessed | tf_op | source)
XLA Modules:
  0.0 27.8 jit_solution(7005883901561018164)
XLA Ops:
  0.0 25.8 %shard_map.73.source = f32[2,256,1,512]{3,2,1,0:T(1,128)} custom-call(f32[2,256,1,512]{3,2,1,0:T(1,128)} %f_in.1, bf16[2,30,120,120]{3,2,1,0:T(8,128)(2,1)} %k_in.1, s32[256,8]{1,0:T(8,128)} %constant.2.clone.tab_in, s32[1,120]{1,0:T(1,128)} %bitcast.1, s32[8,8]{1,0:T(8,128)} %kind_in.1, f32[2]{0:T(128)} %th_in.1, f32[2]{0:T(128)} %rx_in.1), custom_call_target="tpu_custom_call" | custom-call | tf_op jit(solution)/shard_map/pallas_call | solution.py:696
  25.8 2.0 %shard_map.74 = f32[2,256,1,512]{3,2,1,0:T(1,128)} custom-call(f32[2,256,1,512]{3,2,1,0:T(1,128)} %shard_map.73.source), custom_call_target="tpu_custom_call" | custom-call | tf_op jit(solution)/shard_map/pallas_call | solution.py:753
